TPU v7x, 256 devices: a whole 4x4x8 slice. The times are simulated.
256 devices in a mesh: dp: 16 (over y, x), rep: 16 (over z, core).
Axes of the slice: x: 4, y: 4, z: 8, core: 2. Of those that a mesh axis runs over, the one named last changes fastest.
Arguments:
- latent_query_rows: bfloat16 [2048, 64, 512], P(('rep', 'dp')), parts along dimension 0, may hold values from -32 to 32
- rotary_query_parts: bfloat16 [2048, 4096], P(('rep', 'dp')), parts along dimension 0, may hold values from -3 to 3
- latent_cache_rows: bfloat16 [2048, 256, 512], P(('rep', 'dp')), parts along dimension 0, may hold values from -4 to 4
- rotary_cache_keys: bfloat16 [2048, 64, 256], P(('rep', 'dp')), parts along dimension 0, may hold values from -6 to 6
- lengths: int32 [2048], P(('rep', 'dp')), parts along dimension 0, may hold values from 2 to 256, as said below
- adapters: int32 [2048], P(('rep', 'dp')), parts along dimension 0, may hold values from 0 to 63
- value_up_weight: bfloat16 [64, 512, 128], P('dp'), may hold values from -1.5 to 1.5
- output_weight: bfloat16 [8192, 7168], P('dp'), may hold values from -0.0625 to 0.0625
- down_factor_matrix: bfloat16 [8192, 1024], P('dp'), may hold values from -0.0625 to 0.0625
- up_factor_matrix: bfloat16 [16, 64, 7168], P('dp'), may hold values from -1.5 to 1.5
Outputs:
- attn_out: bfloat16 [2048, 7168], P(('rep', 'dp')), parts along dimension 0
There are 16 independent parts, one for each index of `rep`. A program takes and returns all parts, laid end to end along the dimension named above; an argument that names none is the same for every part. Nothing has to cross between parts.
Inputs may be any that keep to these rules, and one draw needn't show every extreme that they name: `lengths`: live cache positions of a request.
All inputs are finite; a program needn't handle non-finite values.
Results may differ from a plain program's by a relative error of at most 0.018.
Values may be sent and summed in bfloat16 or wider, within the bound.
No kernel may reach another device: no remote copies, remote signals or barrier semaphores. Data moves between devices by JAX's collectives and lax.ppermute only.
A program may use at most 64 MiB of HBM per device.

v0:
```python
import jax
import jax.numpy as jnp
from jax import lax
from jax.sharding import PartitionSpec as P

score_scale = 192.0 ** (-0.5)


def on_device(
    latent_query_rows,
    rotary_query_parts,
    latent_cache_rows,
    rotary_cache_keys,
    lengths,
    adapters,
    value_up_weight,
    output_weight,
    down_factor_matrix,
    up_factor_matrix,
):
    req_local, heads, latent = latent_query_rows.shape
    groups = lax.axis_size("dp")
    rope_width = rotary_cache_keys.shape[1]
    cache_len = rotary_cache_keys.shape[2]
    adapter_total = up_factor_matrix.shape[1]
    combined_rank_count = down_factor_matrix.shape[1] // adapter_total
    request_rank_rows = up_factor_matrix.shape[0]
    query_pos = rotary_query_parts.reshape(req_local, heads, rope_width)
    scores = (
        jnp.einsum(
            "rhl,rtl->rht", latent_query_rows, latent_cache_rows, preferred_element_type=jnp.float32
        )
        + jnp.einsum(
            "rhp,rpt->rht", query_pos, rotary_cache_keys, preferred_element_type=jnp.float32
        )
    ) * score_scale
    live_mask = lax.broadcasted_iota(jnp.int32, (1, 1, cache_len), 2) < lengths[:, None, None]
    row_max = jnp.max(jnp.where(live_mask, scores, -jnp.inf), axis=-1, keepdims=True)
    exponent = jnp.where(live_mask, jnp.exp(scores - row_max), 0.0)
    row_total = jnp.sum(exponent, axis=-1, keepdims=True)
    weights = (exponent / row_total).astype(jnp.bfloat16)
    attended = jnp.einsum(
        "rht,rtl->rhl", weights, latent_cache_rows, preferred_element_type=jnp.float32
    ).astype(jnp.bfloat16)
    selection_mask = jax.nn.one_hot(adapters, adapter_total, dtype=jnp.bfloat16)
    spread_hot = jnp.broadcast_to(selection_mask[:, None, :], (req_local, groups, adapter_total))
    gathered, request_selection = (
        lax.all_to_all(attended, "dp", split_axis=1, concat_axis=0, tiled=True),
        lax.all_to_all(spread_hot, "dp", split_axis=1, concat_axis=0, tiled=True),
    )
    all_rows = gathered.shape[0]
    request_selection = request_selection.reshape(all_rows, adapter_total)
    head_value_output = jnp.einsum(
        "rhl,hlv->rhv", gathered, value_up_weight, preferred_element_type=jnp.float32
    )
    head_value_output = head_value_output.astype(jnp.bfloat16).reshape(all_rows, -1)
    projected_output = jnp.dot(
        head_value_output, down_factor_matrix, preferred_element_type=jnp.float32
    ).reshape(all_rows, adapter_total, combined_rank_count)
    partial_low = jnp.sum(
        request_selection.astype(jnp.float32)[:, :, None] * projected_output, axis=1
    )
    low_rank = lax.psum(partial_low, "dp").astype(jnp.bfloat16)
    own_low = lax.dynamic_slice_in_dim(
        low_rank, lax.axis_index("dp") * request_rank_rows, request_rank_rows, 1
    )
    main_sum = lax.psum_scatter(
        jnp.dot(head_value_output, output_weight, preferred_element_type=jnp.float32),
        "dp",
        scatter_dimension=0,
        tiled=True,
    )
    selected_adapter = jnp.dot(
        request_selection, up_factor_matrix[0], preferred_element_type=jnp.float32
    )
    result = own_low.astype(jnp.float32) * selected_adapter
    adapter_sum = lax.psum_scatter(result, "dp", scatter_dimension=0, tiled=True)
    summed = main_sum + adapter_sum
    return summed.astype(jnp.bfloat16)


def solution(mesh):
    placed = (
        P(("rep", "dp"), None, None),
        P(("rep", "dp"), None),
        P(("rep", "dp"), None, None),
        P(("rep", "dp"), None, None),
        P(("rep", "dp")),
        P(("rep", "dp")),
        P("dp", None, None),
        P("dp", None),
        P("dp", None),
        P("dp", None, None),
    )
    return jax.shard_map(
        on_device, mesh=mesh, in_specs=placed, out_specs=P(("rep", "dp"), None), check_vma=False
    )
```

profile of v0, /device:TPU:160, one launch (start us, length us, event | category | flops | bytes accessed | tf_op | source)
XLA Modules:
  0.0 181.3 jit_solution(4348989075300128085)
XLA Ops:
  0.0 0.9 fusion.20
  0.9 0.7 reshape.64
  1.6 7.0 %all-to-all-start.1 = ((bf16[16,2,256]{2,1,0:T(2,128)(2,1)}), bf16[16,2,256]{2,1,0:T(2,128)(2,1)S(1)}, u32[]{:S(2)}, u32[]{:S(2)}) async-start(bf16[16,2,256]{2,1,0:T(2,128)(2,1)} %reshape.64), calls=%async_computation.1 | async-start | bytes 32768 | tf_op jit(solution)/shard_map/all_to_all | solution.py:49
  8.6 1.0 reshape.58
  9.7 0.7 iota_compare_fusion
  10.4 1.8 fusion.29
  12.2 1.2 fusion.5
  13.4 0.8 copy-done.3
  14.2 0.2 fusion.27
  14.4 2.3 %convolution_convert_fusion = bf16[8,64,512]{2,1,0:T(8,128)(2,1)S(1)} fusion(bf16[8,256,512]{2,1,0:T(8,128)(2,1)S(1)} %copy-done, f32[8,64]{1,0:T(8,128)S(1)} %fusion.27, f32[8,64,256]{2,1,0:T(8,128)} %copy-done.3, pred[8,256]{1,0:T(8,128)(4,1)S(1)} %iota_compare_fusion), kind=kOutput, calls=%fused_computation.3 | convolution fusion | flops 135136000 | bytes 3149824 | tf_op jit(solution)/shard_map/rht,rtl->rhl/dot_general | solution.py:42
  16.7 1.1 copy.21
  17.8 7.2 %all-to-all-start = ((bf16[8,64,512]{2,0,1:T(8,128)(2,1)}), bf16[8,64,512]{2,0,1:T(8,128)(2,1)S(1)}, u32[]{:S(2)}, u32[]{:S(2)}) async-start(bf16[8,64,512]{2,0,1:T(8,128)(2,1)} %copy.21), calls=%async_computation | async-start | bytes 1048576 | tf_op jit(solution)/shard_map/all_to_all | solution.py:48
  25.1 2.3 %copy.25 = bf16[512,1024]{0,1:T(8,128)(2,1)} copy(bf16[512,1024]{1,0:T(8,128)(2,1)} %param.18) | data formatting | bytes 2097152 | tf_op args[8]
  27.4 0.6 dynamic-slice
  28.6 0.1 reshape.65
  28.7 0.1 copy.24
  28.8 7.3 %all-to-all-done = bf16[8,64,512]{2,0,1:T(8,128)(2,1)S(1)} async-done(((bf16[8,64,512]{2,0,1:T(8,128)(2,1)}), bf16[8,64,512]{2,0,1:T(8,128)(2,1)S(1)}, u32[]{:S(2)}, u32[]{:S(2)}) %all-to-all-start) | async-done | bytes 524320 | tf_op jit(solution)/shard_map/all_to_all | solution.py:48
  36.0 0.3 convolution_convert_fusion.1
  36.4 2.5 %fusion.6 = f32[128,16]{0,1:T(8,128)S(1)} fusion(bf16[128,512,1]{0,1,2:T(8,128)(2,1)S(1)} %bitcast.50, bf16[64,16,512]{2,1,0:T(8,128)(2,1)} %bitcast.49, f32[128,64]{0,1:T(8,128)S(1)} %copy.24), kind=kOutput, calls=%fused_computation.10 | convolution fusion | flops 134477824 | bytes 1220608 | tf_op jit(solution)/shard_map/dot_general | solution.py:57
  38.9 37.1 %psum.7 = bf16[128,16]{0,1:T(8,128)(2,1)S(1)} all-reduce(f32[128,16]{0,1:T(8,128)S(1)} %fusion.6), channel_id=1, replica_groups=mesh['dp'=16,'rep'=16] {'dp'}, use_global_device_ids=true, to_apply=%region_4.5 | all-reduce | flops 2048 | bytes 12288 | tf_op jit(solution)/shard_map/psum | solution.py:63
  76.0 4.4 %fusion.30 = f32[128,7168]{1,0:T(8,128)S(1)} fusion(bf16[128,512]{0,1:T(8,128)(2,1)S(1)} %bitcast.51, bf16[512,7168]{1,0:T(8,128)(2,1)} %param.17), kind=kOutput, calls=%fused_computation.38 | convolution fusion | flops 939524096 | bytes 11141120 | tf_op jit(solution)/shard_map/dot_general | solution.py:68
  80.4 2.4 %fusion.1 = f32[128,7168]{1,0:T(8,128)} fusion(f32[128,7168]{1,0:T(8,128)S(1)} %fusion.30, f32[128]{0:T(128)S(1)} %fusion.22, bf16[1,64,7168]{2,1,0:T(8,128)(2,1)S(1)} %copy-done.1, bf16[16,8,64]{2,1,0:T(8,128)(2,1)S(1)} %reshape.65), kind=kOutput, calls=%fused_computation.2 | convolution fusion | flops 119275520 | bytes 8274432 | tf_op jit(solution)/shard_map/dot_general | solution.py:73
  82.9 96.9 %all-reduce.2 = bf16[128,7168]{1,0:T(8,128)(2,1)} all-reduce(f32[128,7168]{1,0:T(8,128)} %fusion.1), channel_id=3, replica_groups=mesh['dp'=16,'rep'=16] {'dp'}, use_global_device_ids=true, to_apply=%region_2.3.clone | all-reduce | flops 917504 | bytes 5505024
  179.8 1.6 dynamic-slice_convert_fusion
  (13 shorter events, 0.1 us)
Async XLA Ops:
  0.0 10.4 %copy-start = (bf16[8,256,512]{2,1,0:T(8,128)(2,1)S(1)}, bf16[8,256,512]{2,1,0:T(8,128)(2,1)}, u32[]{:S(2)}) copy-start(bf16[8,256,512]{2,1,0:T(8,128)(2,1)} %param.12) | copy-start | bytes 6291460
  1.6 16.2 %all-to-all-start.1 = ((bf16[16,2,256]{2,1,0:T(2,128)(2,1)}), bf16[16,2,256]{2,1,0:T(2,128)(2,1)S(1)}, u32[]{:S(2)}, u32[]{:S(2)}) async-start(bf16[16,2,256]{2,1,0:T(2,128)(2,1)} %reshape.64), calls=%async_computation.1 | async-start | bytes 32768 | tf_op jit(solution)/shard_map/all_to_all | solution.py:49
  13.4 0.8 copy-start.3
  14.4 13.0 %copy-start.4 = (u32[256]{0:T(256)S(1)}, u32[256]{0:T(256)}, u32[]{:S(2)}) copy-start(u32[256]{0:T(256)} %constant.25) | copy-start | bytes 3076
  14.4 21.6 %copy-start.2 = (bf16[4,512,128]{2,1,0:T(8,128)(2,1)S(1)}, bf16[4,512,128]{2,1,0:T(8,128)(2,1)}, u32[]{:S(2)}) copy-start(bf16[4,512,128]{2,1,0:T(8,128)(2,1)} %param.16) | copy-start | bytes 1572868
  17.8 18.2 %all-to-all-start = ((bf16[8,64,512]{2,0,1:T(8,128)(2,1)}), bf16[8,64,512]{2,0,1:T(8,128)(2,1)S(1)}, u32[]{:S(2)}, u32[]{:S(2)}) async-start(bf16[8,64,512]{2,0,1:T(8,128)(2,1)} %copy.21), calls=%async_computation | async-start | bytes 1048576 | tf_op jit(solution)/shard_map/all_to_all | solution.py:48
  76.0 4.4 %copy-start.1 = (bf16[1,64,7168]{2,1,0:T(8,128)(2,1)S(1)}, bf16[1,64,7168]{2,1,0:T(8,128)(2,1)}, u32[]{:S(2)}) copy-start(bf16[1,64,7168]{2,1,0:T(8,128)(2,1)} %param.19) | copy-start | bytes 2752516
where the time goes:
time: 182 us; the launch traced here: 181 us
  blocking collectives  134 us (74%)
  matrix products  14.9 us (8%)
  starting transfers between devices  14.3 us (8%)
  local copies, waits for them, and re-layouts  8.26 us (5%)
  waiting for transfers between devices  7.25 us (4%)
  other arithmetic  1.87 us (1%)
    unnamed x1, blocking collectives  96.9 us
    psum x1, blocking collectives, on_device(): low_rank = lax.psum(partial_low, 'dp').astype(jnp.bfloat16)  37.1 us
    all_to_all x1, waiting for transfers between devices, on_device(): lax.all_to_all(attended, 'dp', split_axis=1, concat_axis=0, tiled=True)  7.25 us
    all_to_all x1, starting transfers between devices, on_device(): lax.all_to_all(attended, 'dp', split_axis=1, concat_axis=0, tiled=True)  7.22 us
    all_to_all x1, starting transfers between devices, on_device(): lax.all_to_all(spread_hot, 'dp', split_axis=1, concat_axis=0, tiled=True)  7.03 us
    unnamed x15, local copies, waits for them, and re-layouts  4.49 us
    dot_general x1, matrix products, on_device(): jnp.dot(head_value_output, output_weight, preferred_element_type=jnp.floa...  4.39 us
  transfers between devices with their start and end apart: 2, of which 1 were waited for; matrix products, arithmetic and copies ran while one was open for 6% of the time, Pallas kernels for 0%

commit v1 on v0

v1 whole, which is shorter than its diff:
```python
import functools

import jax
import jax.numpy as jnp
from jax import lax
from jax.experimental import pallas as pl
from jax.experimental.pallas import tpu as pltpu
from jax.sharding import PartitionSpec as P

score_scale = 192.0 ** (-0.5)
LANES = 128
F32, BF16 = jnp.float32, jnp.bfloat16


def attention_kernel(
    lengths_ref, adapters_ref, query_ref, rotary_ref, cache_ref, keys_ref, out_ref, rows, attended
):
    req_local = rotary_ref.shape[0]
    heads = query_ref.shape[1]
    rope = keys_ref.shape[1]
    cache_len, latent = cache_ref.shape[1:]
    groups = out_ref.shape[0]
    per_group = heads // groups
    per_step = query_ref.shape[0]
    step = pl.program_id(0)

    @pl.when(step == 0)
    def _():
        for pair in range(heads * rope // LANES):
            slab = rotary_ref[:, pair * LANES : (pair + 1) * LANES].astype(F32)
            for half in range(LANES // rope):
                head = pair * (LANES // rope) + half
                part = slab if half == 0 else pltpu.roll(slab, LANES - half * rope, 1)
                rows[pl.ds(head, req_local, stride=heads), :] = part

    position = lax.broadcasted_iota(jnp.int32, (1, cache_len), 1)
    for own in range(per_step):
        request = step * per_step + own
        cache = cache_ref[own]
        start = pl.multiple_of(request * heads, heads)
        query_pos = rows[pl.ds(start, heads), :][:, :rope].astype(BF16)
        scores = lax.dot_general(
            query_ref[own], cache, (((1,), (1,)), ((), ())), preferred_element_type=F32
        ) + jnp.dot(query_pos, keys_ref[own], preferred_element_type=F32)
        scores = scores * score_scale
        live = position < lengths_ref[request]
        row_max = jnp.max(jnp.where(live, scores, -jnp.inf), axis=-1, keepdims=True)
        exponent = jnp.where(live, jnp.exp(scores - row_max), 0.0)
        row_total = jnp.sum(exponent, axis=-1, keepdims=True)
        weights = (exponent / row_total).astype(BF16)
        mixed = jnp.dot(weights, cache, preferred_element_type=F32)
        for part in range(latent // LANES):
            attended[part, pl.ds(start, heads), :] = mixed[:, part * LANES : (part + 1) * LANES]

    @pl.when(step == pl.num_programs(0) - 1)
    def _():
        for group in range(groups):
            for own in range(per_group):
                picked = pl.ds(group * per_group + own, req_local, stride=heads)
                for part in range(latent // LANES):
                    column = own * latent + part * LANES
                    out_ref[group, :, column : column + LANES] = attended[part, picked, :].astype(
                        BF16
                    )
        row = lax.broadcasted_iota(jnp.int32, (req_local, LANES), 0)
        ids = jnp.zeros((req_local, LANES), jnp.int32)
        for request in range(req_local):
            ids = jnp.where(row == request, adapters_ref[request], ids)
        ids = ids.astype(F32).astype(BF16)
        for group in range(groups):
            out_ref[group, :, per_group * latent :] = ids


def attention(query, rotary, cache, keys, lengths, adapters, groups):
    req_local, heads, latent = query.shape
    rope, cache_len = keys.shape[1:]
    per_step = 2
    width = heads // groups * latent + LANES
    return pl.pallas_call(
        attention_kernel,
        grid=(req_local // per_step,),
        in_specs=[
            pl.BlockSpec(memory_space=pltpu.SMEM),
            pl.BlockSpec(memory_space=pltpu.SMEM),
            pl.BlockSpec((per_step, heads, latent), lambda i: (i, 0, 0)),
            pl.BlockSpec((req_local, heads * rope), lambda i: (0, 0)),
            pl.BlockSpec((per_step, cache_len, latent), lambda i: (i, 0, 0)),
            pl.BlockSpec((per_step, rope, cache_len), lambda i: (i, 0, 0)),
        ],
        out_specs=pl.BlockSpec((groups, req_local, width), lambda i: (0, 0, 0)),
        out_shape=jax.ShapeDtypeStruct((groups, req_local, width), BF16),
        scratch_shapes=[
            pltpu.VMEM((req_local * heads, LANES), F32),
            pltpu.VMEM((latent // LANES, req_local * heads, LANES), F32),
        ],
        compiler_params=pltpu.CompilerParams(vmem_limit_bytes=16 << 20),
        name="attention",
    )(lengths, adapters, query, rotary, cache, keys)


def values_kernel(gathered_ref, up_ref, down_ref, values_ref, low_ref, ids_ref):
    heads, latent, width = up_ref.shape
    all_rows = gathered_ref.shape[0]
    columns = down_ref.shape[1]
    ranks = low_ref.shape[0]
    for head in range(heads):
        values_ref[:, head * width : (head + 1) * width] = jnp.dot(
            gathered_ref[:, head * latent : (head + 1) * latent],
            up_ref[head],
            preferred_element_type=F32,
        ).astype(BF16)
    ids = gathered_ref[:, heads * latent :].astype(F32)
    ids_ref[...] = ids.T[:1]
    projected = jnp.dot(values_ref[...], down_ref[...], preferred_element_type=F32)
    column = lax.broadcasted_iota(jnp.int32, (all_rows, columns), 1)
    picked = jnp.where(column // ranks == ids[:, :1].astype(jnp.int32), projected, 0.0)
    folded = picked[:, :LANES]
    for part in range(1, columns // LANES):
        folded = folded + picked[:, part * LANES : (part + 1) * LANES]
    shift = LANES // 2
    while shift >= ranks:
        folded = folded + pltpu.roll(folded, shift, 1)
        shift //= 2
    low_ref[...] = folded.T[:ranks]


def head_values(gathered, value_up, down, ranks):
    all_rows = gathered.shape[0]
    return pl.pallas_call(
        values_kernel,
        out_shape=(
            jax.ShapeDtypeStruct((all_rows, down.shape[0]), BF16),
            jax.ShapeDtypeStruct((ranks, all_rows), F32),
            jax.ShapeDtypeStruct((1, all_rows), F32),
        ),
        compiler_params=pltpu.CompilerParams(vmem_limit_bytes=16 << 20),
        name="head_values",
    )(gathered, value_up, down)


def project_kernel(values_ref, low_ref, ids_ref, weight_ref, up_ref, out_ref):
    adapter_total = up_ref.shape[0]
    all_rows = values_ref.shape[0]
    low = jnp.sum(low_ref[...], axis=0, keepdims=True)
    adapter = lax.broadcasted_iota(jnp.int32, (adapter_total, all_rows), 0)
    chosen = jnp.where(adapter == ids_ref[...].astype(jnp.int32), low, 0.0).astype(BF16)
    total = jnp.dot(values_ref[...], weight_ref[...], preferred_element_type=F32)
    total = total + lax.dot_general(
        chosen, up_ref[...], (((0,), (0,)), ((), ())), preferred_element_type=F32
    )
    out_ref[...] = total.astype(BF16)


def project(values, low, ids, weight, up):
    all_rows, depth = values.shape
    width = weight.shape[1]
    tile = 1024
    whole = lambda a: pl.BlockSpec(a.shape, lambda i: (0, 0))
    return pl.pallas_call(
        project_kernel,
        grid=(width // tile,),
        in_specs=[
            whole(values),
            whole(low),
            whole(ids),
            pl.BlockSpec((depth, tile), lambda i: (0, i)),
            pl.BlockSpec((up.shape[0], tile), lambda i: (0, i)),
        ],
        out_specs=pl.BlockSpec((all_rows, tile), lambda i: (0, i)),
        out_shape=jax.ShapeDtypeStruct((all_rows, width), BF16),
        compiler_params=pltpu.CompilerParams(vmem_limit_bytes=16 << 20),
        name="project",
    )(values, low, ids, weight, up)


def on_device(
    latent_query_rows,
    rotary_query_parts,
    latent_cache_rows,
    rotary_cache_keys,
    lengths,
    adapters,
    value_up_weight,
    output_weight,
    down_factor_matrix,
    up_factor_matrix,
):
    groups = lax.axis_size("dp")
    exchange = functools.partial(
        lax.all_to_all, axis_name="dp", split_axis=0, concat_axis=0, tiled=True
    )
    adapter_total = up_factor_matrix.shape[1]
    ranks = down_factor_matrix.shape[1] // adapter_total
    message = attention(
        latent_query_rows,
        rotary_query_parts,
        latent_cache_rows,
        rotary_cache_keys,
        lengths,
        adapters,
        groups,
    )
    gathered = exchange(message)
    gathered = gathered.reshape(-1, gathered.shape[-1])
    values, low, ids = head_values(gathered, value_up_weight, down_factor_matrix, ranks)
    low = exchange(low)
    partial = project(values, low, ids, output_weight, up_factor_matrix[0])
    parts = exchange(partial.reshape(groups, -1, partial.shape[-1]))
    return jnp.sum(parts.astype(F32), axis=0).astype(BF16)


def solution(mesh):
    placed = (
        P(("rep", "dp"), None, None),
        P(("rep", "dp"), None),
        P(("rep", "dp"), None, None),
        P(("rep", "dp"), None, None),
        P(("rep", "dp")),
        P(("rep", "dp")),
        P("dp", None, None),
        P("dp", None),
        P("dp", None),
        P("dp", None, None),
    )
    return jax.shard_map(
        on_device, mesh=mesh, in_specs=placed, out_specs=P(("rep", "dp"), None), check_vma=False
    )
```

time: 182 us -> 75.8 us (0.42)
  blocking collectives: 134 us -> 55.6 us
  matrix products: 14.9 us -> 0 us
  starting transfers between devices: 14.3 us -> 0 us
  Pallas kernels: 0 us -> 9.99 us
  waiting for transfers between devices: 7.25 us -> 0 us
    unnamed x1 -> x0, blocking collectives: 96.9 us -> none
    all_to_all x0 -> x3, blocking collectives: none -> 55.6 us  [the longest x1 26 us: on_device(): parts = exchange(partial.reshape(groups, -1, partial.shape[-1]))]
    psum x1 -> x0, blocking collectives: 37.1 us -> none  [on_device(): low_rank = lax.psum(partial_low, 'dp').astype(jnp.bfloat16)]
    dot_general x7 -> x0, matrix products: 14.9 us -> none  [the longest x1 4.39 us: on_device(): jnp.dot(head_value_output, output_weight, preferred_element_type=jnp.floa...]
    all_to_all x2 -> x0, starting transfers between devices: 14.3 us -> none  [the longest x1 7.22 us: on_device(): lax.all_to_all(attended, 'dp', split_axis=1, concat_axis=0, tiled=True)]
    pallas_call x0 -> x3, Pallas kernels: none -> 9.99 us  [the longest x1 5.69 us: attention(): pl.pallas_call(attention_kernel, grid=(req_local // per_step,), in_specs=...]
    all_to_all x2 -> x0, waiting for transfers between devices: 7.25 us -> none  [the longest x1 7.25 us: on_device(): lax.all_to_all(attended, 'dp', split_axis=1, concat_axis=0, tiled=True)]
    unnamed x15 -> x20, local copies, waits for them, and re-layouts: 4.49 us -> 8.83 us
  transfers between devices with their start and end apart: 2 -> 0, of which waited for: 1 -> 0; matrix products, arithmetic and copies ran while one was open for 6% -> 0% of each run, Pallas kernels for 0% -> 0%
where the time goes in v1:
time: 75.8 us; the launch traced here: 75.4 us
  blocking collectives  55.6 us (73%)
  Pallas kernels  9.99 us (13%)
  local copies, waits for them, and re-layouts  8.83 us (12%)
  other arithmetic  0.91 us (1%)
    all_to_all x1, blocking collectives, on_device(): parts = exchange(partial.reshape(groups, -1, partial.shape[-1]))  26 us
    all_to_all x1, blocking collectives, on_device(): gathered = exchange(message)  19 us
    all_to_all x1, blocking collectives, on_device(): low = exchange(low)  10.6 us
    unnamed x20, local copies, waits for them, and re-layouts  8.83 us
    pallas_call x1, Pallas kernels, attention(): pl.pallas_call(attention_kernel, grid=(req_local // per_step,), in_specs=...  5.69 us
    pallas_call x1, Pallas kernels, project(): pl.pallas_call(project_kernel, grid=(width // tile,), in_specs=[whole(val...  3.51 us

profile of v1, /device:TPU:160, one launch (start us, length us, event | category | flops | bytes accessed | tf_op | source)
XLA Modules:
  0.0 75.4 jit_solution(10211445307009313295)
XLA Ops:
  0.0 0.0 copy-start.1
  0.0 1.6 %copy-done.1 = bf16[8,256,512]{2,1,0:T(8,128)(2,1)S(1)} copy-done((bf16[8,256,512]{2,1,0:T(8,128)(2,1)S(1)}, bf16[8,256,512]{2,1,0:T(8,128)(2,1)}, u32[]{:S(2)}) %copy-start.1) | copy-done | bytes 2097176
  1.6 0.0 copy-start.4
  1.6 1.0 %copy-done.4 = bf16[8,64,512]{2,1,0:T(8,128)(2,1)S(1)} copy-done((bf16[8,64,512]{2,1,0:T(8,128)(2,1)S(1)}, bf16[8,64,512]{2,1,0:T(8,128)(2,1)}, u32[]{:S(2)}) %copy-start.4) | copy-done | bytes 524312
  2.6 0.0 copy-start.6
  2.6 0.9 %copy-done.6 = bf16[8,64,256]{2,1,0:T(8,128)(2,1)S(1)} copy-done((bf16[8,64,256]{2,1,0:T(8,128)(2,1)S(1)}, bf16[8,64,256]{2,1,0:T(8,128)(2,1)}, u32[]{:S(2)}) %copy-start.6) | copy-done | bytes 262168
  3.6 0.0 copy-start.7
  3.6 0.8 %copy-done.7 = bf16[8,4096]{1,0:T(8,128)(2,1)S(1)} copy-done((bf16[8,4096]{1,0:T(8,128)(2,1)S(1)}, bf16[8,4096]{1,0:T(8,128)(2,1)}, u32[]{:S(2)}) %copy-start.7) | copy-done | bytes 65560
  4.4 0.0 copy-start.8
  4.4 0.7 copy-done.8
  5.1 0.0 copy-start.9
  5.1 0.7 copy-done.9
  5.7 5.7 %attention.1 = bf16[16,8,2176]{2,1,0:T(8,128)(2,1)S(1)} custom-call(s32[8]{0:T(128)S(1)} %copy-done.8, s32[8]{0:T(128)S(1)} %copy-done.9, bf16[8,64,512]{2,1,0:T(8,128)(2,1)S(1)} %copy-done.4, bf16[8,4096]{1,0:T(8,128)(2,1)S(1)} %copy-done.7, bf16[8,256,512]{2,1,0:T(8,128)(2,1)S(1)} %copy-done.1, bf16[8,64,256]{2,1,0:T(8,128)(2,1)S(1)} %copy-done.6), custom_call_target="tpu_custom_call" | custom-call | tf_op jit(solution)/shard_map/attention/pallas_call | solution.py:79
  11.4 0.0 copy-start.3
  11.4 19.0 %all_to_all.21 = bf16[16,8,2176]{2,1,0:T(8,128)(2,1)S(1)} all-to-all(bf16[16,8,2176]{2,1,0:T(8,128)(2,1)S(1)} %attention.1), channel_id=1, replica_groups=mesh['dp'=16,'rep'=16] {'dp'}, dimensions={0} | all-to-all | bytes 1114112 | tf_op jit(solution)/shard_map/all_to_all | solution.py:203
  30.4 0.0 copy-done.2
  30.4 0.0 copy-done.5
  30.4 0.8 %head_values.1 = (bf16[128,512]{1,0:T(8,128)(2,1)S(1)}, f32[16,128]{1,0:T(8,128)S(1)}, f32[1,128]{1,0:T(1,128)S(1)}) custom-call(bf16[128,2176]{1,0:T(8,128)(2,1)S(1)} %bitcast.8, bf16[4,512,128]{2,1,0:T(8,128)(2,1)S(1)} %copy-done.5, bf16[512,1024]{1,0:T(8,128)(2,1)S(1)} %copy-done.2), custom_call_target="tpu_custom_call" | custom-call | tf_op jit(solution)/shard_map/head_values/pallas_call | solution.py:129
  31.2 10.6 %all_to_all.22 = f32[16,1,128]{2,1,0:T(1,128)S(1)} all-to-all(f32[16,1,128]{2,1,0:T(1,128)S(1)} %bitcast.11), channel_id=1, replica_groups=mesh['dp'=16,'rep'=16] {'dp'}, dimensions={0} | all-to-all | bytes 16384 | tf_op jit(solution)/shard_map/all_to_all | solution.py:206
  41.9 0.0 copy-done.3
  41.9 3.1 %copy-done = bf16[512,7168]{1,0:T(8,128)(2,1)S(1)} copy-done((bf16[512,7168]{1,0:T(8,128)(2,1)S(1)}, bf16[512,7168]{1,0:T(8,128)(2,1)}, u32[]{:S(2)}) %copy-start) | copy-done | bytes 7340056
  45.0 3.5 %project.1 = bf16[128,7168]{1,0:T(8,128)(2,1)S(1)} custom-call(bf16[128,512]{1,0:T(8,128)(2,1)S(1)} %get-tuple-element.8.values_ref, f32[16,128]{1,0:T(8,128)S(1)} %bitcast.10, f32[1,128]{1,0:T(1,128)S(1)} %get-tuple-element.10.ids_ref, bf16[512,7168]{1,0:T(8,128)(2,1)S(1)} %copy-done, bf16[64,7168]{1,0:T(8,128)(2,1)S(1)} %bitcast.9), custom_call_target="tpu_custom_call" | custom-call | tf_op jit(solution)/shard_map/project/pallas_call | solution.py:159
  48.5 26.0 %all_to_all.23 = bf16[16,8,7168]{2,1,0:T(8,128)(2,1)S(1)} all-to-all(bf16[16,8,7168]{2,1,0:T(8,128)(2,1)S(1)} %bitcast.7), channel_id=1, replica_groups=mesh['dp'=16,'rep'=16] {'dp'}, dimensions={0} | all-to-all | bytes 3670016 | tf_op jit(solution)/shard_map/all_to_all | solution.py:208
  74.5 0.9 %reduce_sum.12 = bf16[8,7168]{1,0:T(8,128)(2,1)} reduce(bf16[16,8,7168]{2,1,0:T(8,128)(2,1)S(1)} %all_to_all.23, bf16[]{:T(256)} %constant.2.clone.1), dimensions={0}, to_apply=%region_0.0 | reduce | flops 860160 | bytes 1949698 | tf_op jit(solution)/shard_map/reduce_sum | solution.py:209
  (3 shorter events, 0.0 us)
Async XLA Ops:
  0.0 1.6 %copy-start.1 = (bf16[8,256,512]{2,1,0:T(8,128)(2,1)S(1)}, bf16[8,256,512]{2,1,0:T(8,128)(2,1)}, u32[]{:S(2)}) copy-start(bf16[8,256,512]{2,1,0:T(8,128)(2,1)} %cache_ref.1) | copy-start | bytes 6291460
  1.6 1.0 %copy-start.4 = (bf16[8,64,512]{2,1,0:T(8,128)(2,1)S(1)}, bf16[8,64,512]{2,1,0:T(8,128)(2,1)}, u32[]{:S(2)}) copy-start(bf16[8,64,512]{2,1,0:T(8,128)(2,1)} %query_ref.1) | copy-start | bytes 1572868
  2.6 0.9 %copy-start.6 = (bf16[8,64,256]{2,1,0:T(8,128)(2,1)S(1)}, bf16[8,64,256]{2,1,0:T(8,128)(2,1)}, u32[]{:S(2)}) copy-start(bf16[8,64,256]{2,1,0:T(8,128)(2,1)} %keys_ref.1) | copy-start | bytes 786436
  3.6 0.8 %copy-start.7 = (bf16[8,4096]{1,0:T(8,128)(2,1)S(1)}, bf16[8,4096]{1,0:T(8,128)(2,1)}, u32[]{:S(2)}) copy-start(bf16[8,4096]{1,0:T(8,128)(2,1)} %rotary_ref.1) | copy-start | bytes 196612
  4.4 0.7 copy-start.8
  5.1 0.7 copy-start.9
  5.7 24.7 %copy-start.2 = (bf16[512,1024]{1,0:T(8,128)(2,1)S(1)}, bf16[512,1024]{1,0:T(8,128)(2,1)}, u32[]{:S(2)}) copy-start(bf16[512,1024]{1,0:T(8,128)(2,1)} %down_ref.1) | copy-start | bytes 3145732
  5.7 24.7 %copy-start.5 = (bf16[4,512,128]{2,1,0:T(8,128)(2,1)S(1)}, bf16[4,512,128]{2,1,0:T(8,128)(2,1)}, u32[]{:S(2)}) copy-start(bf16[4,512,128]{2,1,0:T(8,128)(2,1)} %up_ref.1) | copy-start | bytes 1572868
  11.4 30.4 %copy-start.3 = (bf16[1,64,7168]{2,1,0:T(8,128)(2,1)S(1)}, bf16[1,64,7168]{2,1,0:T(8,128)(2,1)}, u32[]{:S(2)}) copy-start(bf16[1,64,7168]{2,1,0:T(8,128)(2,1)} %param.19) | copy-start | bytes 2752516
  41.9 3.1 %copy-start = (bf16[512,7168]{1,0:T(8,128)(2,1)S(1)}, bf16[512,7168]{1,0:T(8,128)(2,1)}, u32[]{:S(2)}) copy-start(bf16[512,7168]{1,0:T(8,128)(2,1)} %weight_ref.1) | copy-start | bytes 22020100

commit v2 on v1

v2 whole, which is shorter than its diff:
```python
import functools
import math

import jax
import jax.numpy as jnp
from jax import lax
from jax.experimental import pallas as pl
from jax.experimental.pallas import tpu as pltpu
from jax.sharding import PartitionSpec as P

exponent_scale = 192.0 ** (-0.5) * math.log2(math.e)
LANES = 128
PER_STEP = 4
TILE = 1792
GROUPS = 16
SIDE = 4
F32, BF16 = jnp.float32, jnp.bfloat16


def attention_kernel(
    lengths_ref,
    adapters_ref,
    query_ref,
    rotary_ref,
    cache_ref,
    keys_ref,
    out_ref,
    rows,
    attended,
):
    req_local = rotary_ref.shape[0]
    heads = query_ref.shape[1]
    rope = keys_ref.shape[1]
    cache_len, latent = cache_ref.shape[1:]
    groups = out_ref.shape[0]
    per_group = heads // groups
    per_step = query_ref.shape[0]
    step = pl.program_id(0)
    @pl.when(step == 0)
    def _():
        for pair in range(heads * rope // LANES):
            slab = rotary_ref[:, pair * LANES : (pair + 1) * LANES].astype(F32)
            for half in range(LANES // rope):
                head = pair * (LANES // rope) + half
                part = slab if half == 0 else pltpu.roll(slab, LANES - half * rope, 1)
                rows[pl.ds(head, req_local, stride=heads), :] = part

    position = lax.broadcasted_iota(jnp.int32, (1, cache_len), 1)
    starts = [pl.multiple_of((step * per_step + own) * heads, heads) for own in range(per_step)]
    scores = []
    for own in range(per_step):
        query_pos = rows[pl.ds(starts[own], heads), :][:, :rope].astype(BF16)
        scores.append(
            lax.dot_general(
                query_ref[own], cache_ref[own], (((1,), (1,)), ((), ())), preferred_element_type=F32
            )
            + jnp.dot(query_pos, keys_ref[own], preferred_element_type=F32)
        )
    weights = []
    for own in range(per_step):
        live = position < lengths_ref[step * per_step + own]
        masked = jnp.where(live, scores[own] * exponent_scale, -jnp.inf)
        exponent = jnp.exp2(masked - jnp.max(masked, axis=-1, keepdims=True))
        row_total = jnp.sum(exponent, axis=-1, keepdims=True)
        weights.append((exponent * (1.0 / row_total)).astype(BF16))
    for own in range(per_step):
        mixed = jnp.dot(weights[own], cache_ref[own], preferred_element_type=F32)
        for part in range(latent // LANES):
            attended[part, pl.ds(starts[own], heads), :] = mixed[:, part * LANES : (part + 1) * LANES]

    @pl.when(step == pl.num_programs(0) - 1)
    def _():
        row = lax.broadcasted_iota(jnp.int32, (req_local, LANES), 0)
        ids = jnp.zeros((req_local, LANES), jnp.int32)
        for request in range(req_local):
            ids = jnp.where(row == request, adapters_ref[request], ids)
        ids = ids.astype(F32).astype(BF16)
        for group in range(groups):
            for own in range(per_group):
                picked = pl.ds(group * per_group + own, req_local, stride=heads)
                for part in range(latent // LANES):
                    column = own * latent + part * LANES
                    out_ref[group, :, column : column + LANES] = attended[part, picked, :].astype(
                        BF16
                    )
            out_ref[group, :, per_group * latent :] = ids


def in_hbm(array):
    return pltpu.with_memory_space_constraint(array, pltpu.HBM)


def attention(query, rotary, cache, keys, lengths, adapters):
    req_local, heads, latent = query.shape
    rope, cache_len = keys.shape[1:]
    per_step = PER_STEP
    width = heads // GROUPS * latent + LANES
    return pl.pallas_call(
        attention_kernel,
        grid=(req_local // per_step,),
        in_specs=[
            pl.BlockSpec(memory_space=pltpu.SMEM),
            pl.BlockSpec(memory_space=pltpu.SMEM),
            pl.BlockSpec((per_step, heads, latent), lambda i: (i, 0, 0)),
            pl.BlockSpec((req_local, heads * rope), lambda i: (0, 0)),
            pl.BlockSpec((per_step, cache_len, latent), lambda i: (i, 0, 0)),
            pl.BlockSpec((per_step, rope, cache_len), lambda i: (i, 0, 0)),
        ],
        out_specs=pl.BlockSpec((GROUPS, req_local, width), lambda i: (0, 0, 0)),
        out_shape=jax.ShapeDtypeStruct((GROUPS, req_local, width), BF16),
        scratch_shapes=[
            pltpu.VMEM((req_local * heads, LANES), F32),
            pltpu.VMEM((latent // LANES, req_local * heads, LANES), F32),
        ],
        compiler_params=pltpu.CompilerParams(vmem_limit_bytes=16 << 20),
        name="attention",
    )(*map(in_hbm, (lengths, adapters, query, rotary, cache, keys)))


def class_of(index):
    return (index // SIDE + index % SIDE) % 2


MEMBERS = [[i for i in range(GROUPS) if class_of(i) == which] for which in range(2)]


def across_x(index, core):
    y, x = index // SIDE, index % SIDE
    step = -1 if (x % 2 == 1) == (core == 0) else 1
    return y * SIDE + (x + step) % SIDE


def across_y(index, core):
    y, x = index // SIDE, index % SIDE
    step = -1 if (y % 2 == 1) == (core == 0) else 1
    return (y + step) % SIDE * SIDE + x


def own_class():
    index = lax.axis_index("dp")
    return lax.rem(index // SIDE + lax.rem(index, SIDE), 2)


def own_core():
    return lax.rem(lax.axis_index("rep"), 2)


def by_class(rows):
    each = rows.shape[0] // GROUPS
    return [
        jnp.concatenate([rows[i * each : (i + 1) * each] for i in members], axis=0)
        for members in MEMBERS
    ]


def project_kernel(
    gathered_ref,
    up_ref,
    down_ref,
    weight_ref,
    low_ref,
    ids_ref,
    own_ref,
    first_ref,
    second_ref,
    up,
    down,
    weight,
    values,
    arrived,
):
    tiles = weight.shape[0]
    copies = [
        pltpu.make_async_copy(up_ref, up, arrived.at[0]),
        pltpu.make_async_copy(down_ref, down, arrived.at[1]),
    ] + [
        pltpu.make_async_copy(
            weight_ref.at[:, tile * TILE : (tile + 1) * TILE],
            weight.at[tile],
            arrived.at[2 + tile],
        )
        for tile in range(tiles)
    ]
    for copy in copies[:3]:
        copy.start()
    heads, latent, width = up.shape
    all_rows = gathered_ref.shape[0]
    columns = down.shape[1]
    ranks = GROUPS
    own_rows = all_rows // 2
    parity, core = own_class(), own_core()
    copies[0].wait()
    for copy in copies[3:]:
        copy.start()
    for head in range(heads):
        result = jnp.dot(
            gathered_ref[:, head * latent : (head + 1) * latent],
            up[head],
            preferred_element_type=F32,
        )
        for which, part in enumerate(by_class(result)):
            values[which, :, head * width : (head + 1) * width] = part.astype(BF16)
    ids = jnp.concatenate(by_class(gathered_ref[:, heads * latent :].astype(F32)), axis=0)
    copies[1].wait()
    projected = jnp.dot(
        values[...].reshape(all_rows, heads * width), down[...], preferred_element_type=F32
    )
    column = lax.broadcasted_iota(jnp.int32, (all_rows, columns), 1)
    picked = jnp.where(column // ranks == ids[:, :1].astype(jnp.int32), projected, 0.0)
    folded = picked[:, :LANES]
    for part in range(1, columns // LANES):
        folded = folded + picked[:, part * LANES : (part + 1) * LANES]
    shift = LANES // 2
    while shift >= ranks:
        folded = folded + pltpu.roll(folded, shift, 1)
        shift //= 2
    low = folded.T[:ranks]
    first = (low, pltpu.roll(low, LANES // 2, 1))
    for index in range(GROUPS):
        chosen = first[class_of(index)]
        pair = [chosen[rank : rank + 1] for rank in (across_y(index, 0), across_y(index, 1))]
        low_ref[index, 0:1, :] = chosen[index : index + 1]
        low_ref[index, 1:2, :] = jnp.where(core == 0, *pair)
    ids = ids.T[:8]
    ids_ref[...] = jnp.where(parity == 0, ids, pltpu.roll(ids, LANES // 2, 1))

    ordered = jnp.concatenate([values[1 - parity], values[parity]], axis=0)
    for tile in range(tiles):
        copies[2 + tile].wait()
        total = jnp.dot(ordered, weight[tile], preferred_element_type=F32)
        other_ref = (first_ref, second_ref)[tile // (tiles // 2)]
        part = tile % (tiles // 2)
        other_ref[:, part * TILE : (part + 1) * TILE] = total[:own_rows].astype(BF16)
        own_ref[:, tile * TILE : (tile + 1) * TILE] = total[own_rows:]


def project(gathered, value_up, down, weight):
    in_vmem = pl.BlockSpec(memory_space=pltpu.VMEM)
    rows, (depth, width) = gathered.shape[0], weight.shape
    tiles = width // TILE
    return pl.pallas_call(
        project_kernel,
        in_specs=[in_vmem] + [pl.BlockSpec(memory_space=pl.ANY)] * 3,
        out_specs=[in_vmem] * 5,
        out_shape=[
            jax.ShapeDtypeStruct((GROUPS, 2, LANES), F32),
            jax.ShapeDtypeStruct((8, LANES), F32),
            jax.ShapeDtypeStruct((rows // 2, width), F32),
            jax.ShapeDtypeStruct((rows // 2, width // 2), BF16),
            jax.ShapeDtypeStruct((rows // 2, width // 2), BF16),
        ],
        scratch_shapes=[
            pltpu.VMEM(value_up.shape, BF16),
            pltpu.VMEM(down.shape, BF16),
            pltpu.VMEM((tiles, depth, TILE), BF16),
            pltpu.VMEM((2, rows // 2, depth), BF16),
            pltpu.SemaphoreType.DMA((2 + tiles,)),
        ],
        compiler_params=pltpu.CompilerParams(vmem_limit_bytes=32 << 20),
        name="project",
    )(gathered, *map(in_hbm, (value_up, down, weight)))


def adapt_kernel(
    low_ref,
    ids_ref,
    own_ref,
    up_ref,
    other_up_ref,
    first_ref,
    second_ref,
    out_ref,
    ups,
    own,
    received,
    arrived,
):
    tiles = ups.shape[0]
    adapter_total = up_ref.shape[0]
    own_rows = own_ref.shape[0]
    copies = []
    for tile in range(tiles):
        columns = pl.ds(tile * TILE, TILE)
        here = pl.ds(tile % (tiles // 2) * TILE, TILE)
        received_ref = (first_ref, second_ref)[tile // (tiles // 2)]
        pairs = (
            (up_ref.at[:, columns], ups.at[tile, pl.ds(0, adapter_total)]),
            (other_up_ref.at[:, columns], ups.at[tile, pl.ds(adapter_total, adapter_total)]),
            (own_ref.at[:, columns], own.at[tile]),
            (received_ref.at[:, here], received.at[tile]),
        )
        copies.append(
            [
                pltpu.make_async_copy(source, target, arrived.at[tile, i])
                for i, (source, target) in enumerate(pairs)
            ]
        )
        for copy in copies[-1]:
            copy.start()
    low = jnp.sum(low_ref[...], axis=0)[:, :own_rows]
    adapter = lax.broadcasted_iota(jnp.int32, (adapter_total, own_rows), 0)
    mine = adapter == ids_ref[:1, :own_rows].astype(jnp.int32)
    chosen = jnp.concatenate(
        [jnp.where(mine, low[slot : slot + 1], 0.0) for slot in range(2)], axis=0
    )
    chosen = chosen.T.astype(BF16)
    for tile in range(tiles):
        for copy in copies[tile]:
            copy.wait()
        total = own[tile] + received[tile].astype(F32)
        total = total + jnp.dot(chosen, ups[tile], preferred_element_type=F32)
        out_ref[:, tile * TILE : (tile + 1) * TILE] = total.astype(BF16)


def adapt(low, ids, own, up, other_up, received):
    in_vmem = pl.BlockSpec(memory_space=pltpu.VMEM)
    rows, width = own.shape
    tiles = width // TILE
    return pl.pallas_call(
        adapt_kernel,
        in_specs=[in_vmem] * 2 + [pl.BlockSpec(memory_space=pl.ANY)] * 5,
        out_specs=in_vmem,
        out_shape=jax.ShapeDtypeStruct(own.shape, BF16),
        scratch_shapes=[
            pltpu.VMEM((tiles, 2 * up.shape[0], TILE), BF16),
            pltpu.VMEM((tiles, rows, TILE), F32),
            pltpu.VMEM((tiles, rows, TILE), BF16),
            pltpu.SemaphoreType.DMA((tiles, 4)),
        ],
        compiler_params=pltpu.CompilerParams(vmem_limit_bytes=16 << 20),
        name="adapt",
    )(low, ids, own, in_hbm(up), other_up, *received)


def on_device(
    latent_query_rows,
    rotary_query_parts,
    latent_cache_rows,
    rotary_cache_keys,
    lengths,
    adapters,
    value_up_weight,
    output_weight,
    down_factor_matrix,
    up_factor_matrix,
):
    exchange = functools.partial(
        lax.all_to_all, axis_name="dp", split_axis=0, concat_axis=0, tiled=True
    )
    replicas = lax.axis_size("rep")
    swap = lambda array, partner: lax.ppermute(
        array,
        ("dp", "rep"),
        [
            (index * replicas + rep, partner(index, rep % 2) * replicas + rep)
            for index in range(GROUPS)
            for rep in range(replicas)
        ],
    )
    up = up_factor_matrix[0]
    other_up = swap(up, across_y)
    message = attention(
        latent_query_rows,
        rotary_query_parts,
        latent_cache_rows,
        rotary_cache_keys,
        lengths,
        adapters,
    )
    gathered = exchange(message)
    gathered = gathered.reshape(-1, gathered.shape[-1])
    low, ids, own, *others = project(
        gathered, value_up_weight, down_factor_matrix, output_weight
    )
    received = [
        swap(part, lambda index, _, half=half: across_x(index, half))
        for half, part in enumerate(others)
    ]
    low = exchange(low)
    partial = adapt(low, ids, own, up, other_up, received)
    parts = exchange(
        partial.reshape(GROUPS // 2, -1, partial.shape[-1]), axis_index_groups=MEMBERS
    )
    return jnp.sum(parts.astype(F32), axis=0).astype(BF16)


def solution(mesh):
    placed = (
        P(("rep", "dp"), None, None),
        P(("rep", "dp"), None),
        P(("rep", "dp"), None, None),
        P(("rep", "dp"), None, None),
        P(("rep", "dp")),
        P(("rep", "dp")),
        P("dp", None, None),
        P("dp", None),
        P("dp", None),
        P("dp", None, None),
    )
    return jax.shard_map(
        on_device, mesh=mesh, in_specs=placed, out_specs=P(("rep", "dp"), None), check_vma=False
    )
```

time: 75.8 us -> 61.4 us (0.81)
  blocking collectives: 55.6 us -> 28.1 us
  starting transfers between devices: 0 us -> 10.9 us
  waiting for transfers between devices: 0 us -> 9.92 us
  local copies, waits for them, and re-layouts: 8.83 us -> 0.01 us
  Pallas kernels: 9.99 us -> 11.4 us
    all_to_all x2 -> x1, blocking collectives: 45 us -> 16.7 us  [on_device(): exchange(partial.reshape(GROUPS // 2, -1, partial.shape[-1]), axis_index_...]
    all_to_all x0 -> x1, waiting for transfers between devices: none -> 9.91 us  [on_device(): gathered = exchange(message)]
    unnamed x20 -> x2, local copies, waits for them, and re-layouts: 8.83 us -> 0.01 us
    all_to_all x0 -> x1, starting transfers between devices: none -> 7.04 us  [on_device(): gathered = exchange(message)]
    ppermute x0 -> x3, starting transfers between devices: none -> 3.85 us  [on_device(): lax.ppermute(array, ('dp', 'rep'), [(index * replicas + rep, partner(inde...]
    pallas_call x2, Pallas kernels: 4.31 us -> 6.44 us  [the longest x1 4.46 us: project(): pl.pallas_call(project_kernel, in_specs=[in_vmem] + [pl.BlockSpec(memory_...]
    all_to_all x1, blocking collectives: 10.6 us -> 11.4 us  [on_device(): low = exchange(low)]
  transfers between devices with their start and end apart: 0 -> 4, of which waited for: 0 -> 1; matrix products, arithmetic and copies ran while one was open for 0% -> 0% of each run, Pallas kernels for 0% -> 7%
where the time goes in v2:
time: 61.4 us; the launch traced here: 61.2 us
  blocking collectives  28.1 us (46%)
  Pallas kernels  11.4 us (19%)
  starting transfers between devices  10.9 us (18%)
  waiting for transfers between devices  9.92 us (16%)
  other arithmetic  0.78 us (1%)
    all_to_all x1, blocking collectives, on_device(): exchange(partial.reshape(GROUPS // 2, -1, partial.shape[-1]), axis_index_...  16.7 us
    all_to_all x1, blocking collectives, on_device(): low = exchange(low)  11.4 us
    all_to_all x1, waiting for transfers between devices, on_device(): gathered = exchange(message)  9.91 us
    all_to_all x1, starting transfers between devices, on_device(): gathered = exchange(message)  7.04 us
    pallas_call x1, Pallas kernels, attention(): pl.pallas_call(attention_kernel, grid=(req_local // per_step,), in_specs=...  4.94 us
    pallas_call x1, Pallas kernels, project(): pl.pallas_call(project_kernel, in_specs=[in_vmem] + [pl.BlockSpec(memory_...  4.46 us
    ppermute x3, starting transfers between devices, on_device(): lax.ppermute(array, ('dp', 'rep'), [(index * replicas + rep, partner(inde...  3.85 us
    pallas_call x1, Pallas kernels, adapt(): pl.pallas_call(adapt_kernel, in_specs=[in_vmem] * 2 + [pl.BlockSpec(memor...  1.98 us
  transfers between devices with their start and end apart: 4, of which 1 were waited for; matrix products, arithmetic and copies ran while one was open for 0% of the time, Pallas kernels for 7%

profile of v2, /device:TPU:160, one launch (start us, length us, event | category | flops | bytes accessed | tf_op | source)
XLA Modules:
  0.0 61.2 jit_solution(18324581494708073461)
XLA Ops:
  0.0 0.0 copy-start
  0.0 4.9 %attention.1 = bf16[16,8,2176]{2,1,0:T(8,128)(2,1)} custom-call(s32[8]{0:T(128)} %lengths_ref.1, s32[8]{0:T(128)} %adapters_ref.1, bf16[8,64,512]{2,1,0:T(8,128)(2,1)} %query_ref.1, bf16[8,4096]{1,0:T(8,128)(2,1)} %rotary_ref.1, bf16[8,256,512]{2,1,0:T(8,128)(2,1)} %cache_ref.1, bf16[8,64,256]{2,1,0:T(8,128)(2,1)} %keys_ref.1), custom_call_target="tpu_custom_call" | custom-call | tf_op jit(solution)/shard_map/attention/pallas_call | solution.py:98
  4.9 7.0 %all-to-all-start = ((bf16[16,8,2176]{2,1,0:T(8,128)(2,1)}), bf16[16,8,2176]{2,1,0:T(8,128)(2,1)S(1)}, u32[]{:S(2)}, u32[]{:S(2)}) async-start(bf16[16,8,2176]{2,1,0:T(8,128)(2,1)} %attention.1), calls=%async_computation | async-start | bytes 1114112 | tf_op jit(solution)/shard_map/all_to_all | solution.py:370
  12.0 0.0 copy-done
  12.0 2.0 %collective-permute-start = (bf16[64,7168]{1,0:T(8,128)(2,1)S(1)}, bf16[64,7168]{1,0:T(8,128)(2,1)S(1)}, u32[]{:S(2)}, u32[]{:S(2)}) collective-permute-start(bf16[64,7168]{1,0:T(8,128)(2,1)S(1)} %bitcast.6), channel_id=1, source_target_pairs={{0,64},{1,193},{2,66},{3,195},{4,68},{5,197},{6,70},{7,199},{8,72}... | collective-permute-start | bytes 2752520 | tf_op jit(solution)/shard_map/ppermute | solution.py:351
  14.0 9.9 %all-to-all-done = bf16[16,8,2176]{2,1,0:T(8,128)(2,1)S(1)} async-done(((bf16[16,8,2176]{2,1,0:T(8,128)(2,1)}), bf16[16,8,2176]{2,1,0:T(8,128)(2,1)S(1)}, u32[]{:S(2)}, u32[]{:S(2)}) %all-to-all-start) | async-done | bytes 557088 | tf_op jit(solution)/shard_map/all_to_all | solution.py:370
  23.9 4.5 %project.1 = (f32[16,2,128]{2,1,0:T(2,128)S(1)}, f32[8,128]{1,0:T(8,128)S(1)}, f32[64,7168]{1,0:T(8,128)S(1)}, bf16[64,3584]{1,0:T(8,128)(2,1)S(1)}, bf16[64,3584]{1,0:T(8,128)(2,1)S(1)}) custom-call(bf16[128,2176]{1,0:T(8,128)(2,1)S(1)} %bitcast.4, bf16[4,512,128]{2,1,0:T(8,128)(2,1)} %up_ref.1, bf16[512,1024]{1,0:T(8,128)(2,1)} %down_ref.1, ...), custom_call_target="tpu_custom_call" | custom-call | tf_op jit(solution)/shard_map/project/pallas_call | solution.py:241
  28.4 0.7 %collective-permute-start.1 = (bf16[64,3584]{1,0:T(8,128)(2,1)S(1)}, bf16[64,3584]{1,0:T(8,128)(2,1)S(1)}, u32[]{:S(2)}, u32[]{:S(2)}) collective-permute-start(bf16[64,3584]{1,0:T(8,128)(2,1)S(1)} %get-tuple-element.13), channel_id=1, source_target_pairs={{0,16},{1,17},{2,18},{3,19},{4,20},{5,21},{6,22},{7,23},{8,24},{9,... | collective-permute-start | bytes 1376264 | tf_op jit(solution)/shard_map/ppermute | solution.py:351
  29.0 1.2 %collective-permute-start.2 = (bf16[64,3584]{1,0:T(8,128)(2,1)S(1)}, bf16[64,3584]{1,0:T(8,128)(2,1)S(1)}, u32[]{:S(2)}, u32[]{:S(2)}) collective-permute-start(bf16[64,3584]{1,0:T(8,128)(2,1)S(1)} %get-tuple-element.14), channel_id=1, source_target_pairs={{0,48},{1,49},{2,50},{3,51},{4,52},{5,53},{6,54},{7,55},{8,56},{9,... | collective-permute-start | bytes 1376264 | tf_op jit(solution)/shard_map/ppermute | solution.py:351
  30.2 11.4 %all_to_all.15.low_ref = f32[16,2,128]{2,1,0:T(2,128)S(1)} all-to-all(f32[16,2,128]{2,1,0:T(2,128)S(1)} %get-tuple-element.10), channel_id=1, replica_groups=mesh['dp'=16,'rep'=16] {'dp'}, dimensions={0} | all-to-all | bytes 32768 | tf_op jit(solution)/shard_map/all_to_all | solution.py:379
  41.7 0.0 collective-permute-done.other_up_ref
  41.7 0.0 collective-permute-done.1.first_ref
  41.7 0.0 collective-permute-done.2.second_ref
  41.7 2.0 %adapt.1 = bf16[64,7168]{1,0:T(8,128)(2,1)S(1)} custom-call(f32[16,2,128]{2,1,0:T(2,128)S(1)} %all_to_all.15.low_ref, f32[8,128]{1,0:T(8,128)S(1)} %get-tuple-element.11.ids_ref, f32[64,7168]{1,0:T(8,128)S(1)} %get-tuple-element.12.own_ref, bf16[64,7168]{1,0:T(8,128)(2,1)} %bitcast.5, bf16[64,7168]{1,0:T(8,128)(2,1)S(1)} %collective-permute-done.other_up_ref, ...), custom_call_target="tpu_custom_call" | custom-call | tf_op jit(solution)/shard_map/adapt/pallas_call | solution.py:319
  43.7 16.7 %all_to_all.16 = bf16[8,8,7168]{2,1,0:T(8,128)(2,1)S(1)} all-to-all(bf16[8,8,7168]{2,1,0:T(8,128)(2,1)S(1)} %bitcast.3), channel_id=1, replica_groups={{0,32,80,112,128,160,208,240},{16,48,64,96,144,176,192,224},{1,33,81,11..., dimensions={0} | all-to-all | bytes 1835008 | tf_op jit(solution)/shard_map/all_to_all | solution.py:381
  60.4 0.8 %reduce_sum.12 = bf16[8,7168]{1,0:T(8,128)(2,1)} reduce(bf16[8,8,7168]{2,1,0:T(8,128)(2,1)S(1)} %all_to_all.16, bf16[]{:T(256)} %constant.2.clone.1), dimensions={0}, to_apply=%region_0.0 | reduce | flops 401408 | bytes 1032194 | tf_op jit(solution)/shard_map/reduce_sum | solution.py:384
Async XLA Ops:
  0.0 12.0 %copy-start = (bf16[1,64,7168]{2,1,0:T(8,128)(2,1)S(1)}, bf16[1,64,7168]{2,1,0:T(8,128)(2,1)}, u32[]{:S(2)}) copy-start(bf16[1,64,7168]{2,1,0:T(8,128)(2,1)} %param.19) | copy-start | bytes 2752516
  4.9 19.0 %all-to-all-start = ((bf16[16,8,2176]{2,1,0:T(8,128)(2,1)}), bf16[16,8,2176]{2,1,0:T(8,128)(2,1)S(1)}, u32[]{:S(2)}, u32[]{:S(2)}) async-start(bf16[16,8,2176]{2,1,0:T(8,128)(2,1)} %attention.1), calls=%async_computation | async-start | bytes 1114112 | tf_op jit(solution)/shard_map/all_to_all | solution.py:370
  12.0 29.7 %collective-permute-start = (bf16[64,7168]{1,0:T(8,128)(2,1)S(1)}, bf16[64,7168]{1,0:T(8,128)(2,1)S(1)}, u32[]{:S(2)}, u32[]{:S(2)}) collective-permute-start(bf16[64,7168]{1,0:T(8,128)(2,1)S(1)} %bitcast.6), channel_id=1, source_target_pairs={{0,64},{1,193},{2,66},{3,195},{4,68},{5,197},{6,70},{7,199},{8,72}... | collective-permute-start | bytes 2752520 | tf_op jit(solution)/shard_map/ppermute | solution.py:351
  28.4 13.3 %collective-permute-start.1 = (bf16[64,3584]{1,0:T(8,128)(2,1)S(1)}, bf16[64,3584]{1,0:T(8,128)(2,1)S(1)}, u32[]{:S(2)}, u32[]{:S(2)}) collective-permute-start(bf16[64,3584]{1,0:T(8,128)(2,1)S(1)} %get-tuple-element.13), channel_id=1, source_target_pairs={{0,16},{1,17},{2,18},{3,19},{4,20},{5,21},{6,22},{7,23},{8,24},{9,... | collective-permute-start | bytes 1376264 | tf_op jit(solution)/shard_map/ppermute | solution.py:351
  29.0 12.6 %collective-permute-start.2 = (bf16[64,3584]{1,0:T(8,128)(2,1)S(1)}, bf16[64,3584]{1,0:T(8,128)(2,1)S(1)}, u32[]{:S(2)}, u32[]{:S(2)}) collective-permute-start(bf16[64,3584]{1,0:T(8,128)(2,1)S(1)} %get-tuple-element.14), channel_id=1, source_target_pairs={{0,48},{1,49},{2,50},{3,51},{4,52},{5,53},{6,54},{7,55},{8,56},{9,... | collective-permute-start | bytes 1376264 | tf_op jit(solution)/shard_map/ppermute | solution.py:351

commit v3 on v2

v3 whole, which is shorter than its diff:
```python
import functools
import math

import jax
import jax.numpy as jnp
from jax import lax
from jax.experimental import pallas as pl
from jax.experimental.pallas import tpu as pltpu
from jax.sharding import PartitionSpec as P

exponent_scale = 192.0 ** (-0.5) * math.log2(math.e)
LANES = 128
PER_STEP = 4
TILE = 1792
GROUPS = 16
SIDE = 4
CLASSES = 4
F32, BF16 = jnp.float32, jnp.bfloat16


def attention_kernel(
    lengths_ref,
    adapters_ref,
    query_ref,
    rotary_ref,
    cache_ref,
    keys_ref,
    weight_in,
    out_ref,
    weight_out,
    rows,
    attended,
    arrived,
):
    staging = pltpu.make_async_copy(weight_in.at[:, :TILE], weight_out, arrived.at[0])
    req_local = rotary_ref.shape[0]
    heads = query_ref.shape[1]
    rope = keys_ref.shape[1]
    cache_len, latent = cache_ref.shape[1:]
    groups = out_ref.shape[0]
    per_group = heads // groups
    per_step = query_ref.shape[0]
    step = pl.program_id(0)
    @pl.when(step == 0)
    def _():
        staging.start()
        for pair in range(heads * rope // LANES):
            slab = rotary_ref[:, pair * LANES : (pair + 1) * LANES].astype(F32)
            for half in range(LANES // rope):
                head = pair * (LANES // rope) + half
                part = slab if half == 0 else pltpu.roll(slab, LANES - half * rope, 1)
                rows[pl.ds(head, req_local, stride=heads), :] = part

    position = lax.broadcasted_iota(jnp.int32, (1, cache_len), 1)
    starts = [pl.multiple_of((step * per_step + own) * heads, heads) for own in range(per_step)]
    scores = []
    for own in range(per_step):
        query_pos = rows[pl.ds(starts[own], heads), :][:, :rope].astype(BF16)
        scores.append(
            lax.dot_general(
                query_ref[own], cache_ref[own], (((1,), (1,)), ((), ())), preferred_element_type=F32
            )
            + jnp.dot(query_pos, keys_ref[own], preferred_element_type=F32)
        )
    weights = []
    for own in range(per_step):
        live = position < lengths_ref[step * per_step + own]
        masked = jnp.where(live, scores[own] * exponent_scale, -jnp.inf)
        exponent = jnp.exp2(masked - jnp.max(masked, axis=-1, keepdims=True))
        row_total = jnp.sum(exponent, axis=-1, keepdims=True)
        weights.append((exponent * (1.0 / row_total)).astype(BF16))
    for own in range(per_step):
        mixed = jnp.dot(weights[own], cache_ref[own], preferred_element_type=F32)
        for part in range(latent // LANES):
            attended[part, pl.ds(starts[own], heads), :] = mixed[:, part * LANES : (part + 1) * LANES]

    @pl.when(step == pl.num_programs(0) - 1)
    def _():
        row = lax.broadcasted_iota(jnp.int32, (req_local, LANES), 0)
        ids = jnp.zeros((req_local, LANES), jnp.int32)
        for request in range(req_local):
            ids = jnp.where(row == request, adapters_ref[request], ids)
        ids = ids.astype(F32).astype(BF16)
        for group in range(groups):
            for own in range(per_group):
                picked = pl.ds(group * per_group + own, req_local, stride=heads)
                for part in range(latent // LANES):
                    column = own * latent + part * LANES
                    out_ref[group, :, column : column + LANES] = attended[part, picked, :].astype(
                        BF16
                    )
            out_ref[group, :, per_group * latent :] = ids
        staging.wait()


def in_hbm(array):
    return pltpu.with_memory_space_constraint(array, pltpu.HBM)


def attention(query, rotary, cache, keys, lengths, adapters, weight):
    req_local, heads, latent = query.shape
    rope, cache_len = keys.shape[1:]
    per_step = PER_STEP
    width = heads // GROUPS * latent + LANES
    anywhere = pl.BlockSpec(memory_space=pl.ANY)
    return pl.pallas_call(
        attention_kernel,
        grid=(req_local // per_step,),
        in_specs=[
            pl.BlockSpec(memory_space=pltpu.SMEM),
            pl.BlockSpec(memory_space=pltpu.SMEM),
            pl.BlockSpec((per_step, heads, latent), lambda i: (i, 0, 0)),
            pl.BlockSpec((req_local, heads * rope), lambda i: (0, 0)),
            pl.BlockSpec((per_step, cache_len, latent), lambda i: (i, 0, 0)),
            pl.BlockSpec((per_step, rope, cache_len), lambda i: (i, 0, 0)),
            anywhere,
        ],
        out_specs=[
            pl.BlockSpec((GROUPS, req_local, width), lambda i: (0, 0, 0)),
            anywhere,
        ],
        out_shape=[
            jax.ShapeDtypeStruct((GROUPS, req_local, width), BF16),
            pltpu.VMEM((weight.shape[0], TILE), BF16),
        ],
        scratch_shapes=[
            pltpu.VMEM((req_local * heads, LANES), F32),
            pltpu.VMEM((latent // LANES, req_local * heads, LANES), F32),
            pltpu.SemaphoreType.DMA((1,)),
        ],
        compiler_params=pltpu.CompilerParams(vmem_limit_bytes=16 << 20),
        name="attention",
    )(*map(in_hbm, (lengths, adapters, query, rotary, cache, keys, weight)))


def class_of(index):
    return (index // SIDE + 2 * (index % SIDE)) % CLASSES


MEMBERS = [[i for i in range(GROUPS) if class_of(i) == which] for which in range(CLASSES)]
PEERS = (2, 9, 11)


def across_x(index, core):
    y, x = index // SIDE, index % SIDE
    step = -1 if (x % 2 == 1) == (core == 0) else 1
    return y * SIDE + (x + step) % SIDE


def along_y(index, step):
    return (index // SIDE + step) % SIDE * SIDE + index % SIDE


def own_place():
    index = lax.axis_index("dp")
    y, x = index // SIDE, lax.rem(index, SIDE)
    return lax.rem(y + 2 * x, CLASSES), 2 * (y // 2) + x // 2


def own_core():
    return lax.rem(lax.axis_index("rep"), 2)


def by_class(rows):
    each = rows.shape[0] // GROUPS
    return [
        jnp.concatenate([rows[i * each : (i + 1) * each] for i in members], axis=0)
        for members in MEMBERS
    ]


def project_kernel(
    gathered_ref,
    first_tile,
    up_ref,
    down_ref,
    weight_ref,
    low_ref,
    ids_ref,
    own_ref,
    above_ref,
    across_ref,
    below_ref,
    up,
    down,
    weight,
    values,
    arrived,
):
    tiles = weight.shape[0] + 1
    copies = [
        pltpu.make_async_copy(up_ref, up, arrived.at[0]),
        pltpu.make_async_copy(down_ref, down, arrived.at[1]),
    ] + [
        pltpu.make_async_copy(
            weight_ref.at[:, tile * TILE : (tile + 1) * TILE],
            weight.at[tile - 1],
            arrived.at[1 + tile],
        )
        for tile in range(1, tiles)
    ]
    for copy in copies:
        copy.start()
    heads, latent, width = up.shape
    all_rows = gathered_ref.shape[0]
    columns = down.shape[1]
    ranks = GROUPS
    own_rows = all_rows // CLASSES
    (which_own, _), core = own_place(), own_core()
    copies[0].wait()
    for head in range(heads):
        result = jnp.dot(
            gathered_ref[:, head * latent : (head + 1) * latent],
            up[head],
            preferred_element_type=F32,
        )
        for which, part in enumerate(by_class(result)):
            values[which, :, head * width : (head + 1) * width] = part.astype(BF16)
    ids = jnp.concatenate(by_class(gathered_ref[:, heads * latent :].astype(F32)), axis=0)
    copies[1].wait()
    projected = jnp.dot(
        values[...].reshape(all_rows, heads * width), down[...], preferred_element_type=F32
    )
    column = lax.broadcasted_iota(jnp.int32, (all_rows, columns), 1)
    picked = jnp.where(column // ranks == ids[:, :1].astype(jnp.int32), projected, 0.0)
    folded = picked[:, :LANES]
    for part in range(1, columns // LANES):
        folded = folded + picked[:, part * LANES : (part + 1) * LANES]
    shift = LANES // 2
    while shift >= ranks:
        folded = folded + pltpu.roll(folded, shift, 1)
        shift //= 2
    low = folded.T[:ranks]
    turns = [(LANES - which * own_rows) % LANES for which in range(CLASSES)]
    turned = [low if turn == 0 else pltpu.roll(low, turn, 1) for turn in turns]
    for index in range(GROUPS):
        chosen = turned[class_of(index)]
        low_ref[index, 0:1, :] = chosen[index : index + 1]
        above, below = along_y(index, 1), along_y(index, -1)
        pairs = ((above, below), (below, above), (across_x(index, 0), across_x(index, 1)))
        for slot, pair in enumerate(pairs):
            pair = [chosen[rank : rank + 1] for rank in pair]
            low_ref[index, slot + 1 : slot + 2, :] = jnp.where(core == 0, *pair)
    ids = ids.T[:8]
    own_ids = ids
    for which in range(1, CLASSES):
        own_ids = jnp.where(which_own == which, pltpu.roll(ids, turns[which], 1), own_ids)
    ids_ref[...] = own_ids

    ordered = jnp.concatenate(
        [values[lax.rem(which_own + step, CLASSES)] for step in (1, 2, 3, 0)], axis=0
    )
    for tile in range(tiles):
        if tile > 0:
            copies[1 + tile].wait()
        part = weight[tile - 1] if tile > 0 else first_tile[...]
        total = jnp.dot(ordered, part, preferred_element_type=F32)
        columns = pl.ds(tile * TILE, TILE)
        for i, other_ref in enumerate((above_ref, across_ref, below_ref)):
            other_ref[:, columns] = total[i * own_rows : (i + 1) * own_rows].astype(BF16)
        own_ref[:, columns] = total[3 * own_rows :]


def project(gathered, first_tile, value_up, down, weight):
    in_vmem = pl.BlockSpec(memory_space=pltpu.VMEM)
    rows, (depth, width) = gathered.shape[0], weight.shape
    tiles = width // TILE
    return pl.pallas_call(
        project_kernel,
        in_specs=[in_vmem] * 2 + [pl.BlockSpec(memory_space=pl.ANY)] * 3,
        out_specs=[in_vmem] * 6,
        out_shape=[
            jax.ShapeDtypeStruct((GROUPS, 4, LANES), F32),
            jax.ShapeDtypeStruct((8, LANES), F32),
            jax.ShapeDtypeStruct((rows // CLASSES, width), F32),
        ]
        + [jax.ShapeDtypeStruct((rows // CLASSES, width), BF16)] * 3,
        scratch_shapes=[
            pltpu.VMEM(value_up.shape, BF16),
            pltpu.VMEM(down.shape, BF16),
            pltpu.VMEM((tiles - 1, depth, TILE), BF16),
            pltpu.VMEM((CLASSES, rows // CLASSES, depth), BF16),
            pltpu.SemaphoreType.DMA((1 + tiles,)),
        ],
        compiler_params=pltpu.CompilerParams(vmem_limit_bytes=32 << 20),
        name="project",
    )(gathered, first_tile, *map(in_hbm, (value_up, down, weight)))


def adapt_kernel(
    low_ref,
    ids_ref,
    own_ref,
    above_ref,
    across_ref,
    below_ref,
    *refs,
):
    up_refs, out_refs, (ups, totals, arrived) = refs[:4], refs[4:8], refs[8:]
    tiles = ups.shape[0]
    own_rows = own_ref.shape[0]
    adapter_total = up_refs[0].shape[0]
    copies = []
    for tile in range(tiles):
        for slot, up_ref in enumerate(up_refs):
            copies.append(
                pltpu.make_async_copy(
                    up_ref.at[:, tile * TILE : (tile + 1) * TILE],
                    ups.at[tile, pl.ds(slot * adapter_total, adapter_total)],
                    arrived.at[tile, slot],
                )
            )
            copies[-1].start()
    low = jnp.sum(low_ref[...], axis=0)[:, :own_rows]
    adapter = lax.broadcasted_iota(jnp.int32, (adapter_total, own_rows), 0)
    mine = adapter == ids_ref[:1, :own_rows].astype(jnp.int32)
    chosen = jnp.concatenate(
        [jnp.where(mine, low[slot : slot + 1], 0.0) for slot in range(4)], axis=0
    )
    chosen = chosen.T.astype(BF16)
    _, place = own_place()
    each = own_rows // CLASSES
    for tile in range(tiles):
        columns = pl.ds(tile * TILE, TILE)
        total = own_ref[:, columns]
        for received_ref in (above_ref, across_ref, below_ref):
            total = total + received_ref[:, columns].astype(F32)
        for copy in copies[4 * tile : 4 * tile + 4]:
            copy.wait()
        total = total + jnp.dot(chosen, ups[tile], preferred_element_type=F32)
        totals[...] = total.reshape(CLASSES, each, TILE)
        for turn, out_ref in enumerate(out_refs):
            out_ref[:, columns] = totals[place ^ turn].astype(BF16)


def adapt(low, ids, own, received, ups):
    in_vmem = pl.BlockSpec(memory_space=pltpu.VMEM)
    near = [pltpu.with_memory_space_constraint(a, pltpu.VMEM) for a in (own, *received)]
    rows, width = own.shape
    tiles = width // TILE
    return pl.pallas_call(
        adapt_kernel,
        in_specs=[in_vmem] * 6 + [pl.BlockSpec(memory_space=pl.ANY)] * 4,
        out_specs=[in_vmem] * 4,
        out_shape=[jax.ShapeDtypeStruct((rows // CLASSES, width), BF16)] * 4,
        scratch_shapes=[
            pltpu.VMEM((tiles, 4 * ups[0].shape[0], TILE), BF16),
            pltpu.VMEM((CLASSES, rows // CLASSES, TILE), F32),
            pltpu.SemaphoreType.DMA((tiles, 4)),
        ],
        compiler_params=pltpu.CompilerParams(vmem_limit_bytes=16 << 20),
        name="adapt",
    )(low, ids, *near, in_hbm(ups[0]), *ups[1:])


def on_device(
    latent_query_rows,
    rotary_query_parts,
    latent_cache_rows,
    rotary_cache_keys,
    lengths,
    adapters,
    value_up_weight,
    output_weight,
    down_factor_matrix,
    up_factor_matrix,
):
    exchange = functools.partial(
        lax.all_to_all, axis_name="dp", split_axis=0, concat_axis=0, tiled=True
    )
    replicas = lax.axis_size("rep")

    def swap(array, partner):
        pairs = [
            (index * replicas + rep, partner(index, rep))
            for index in range(GROUPS)
            for rep in range(replicas)
        ]
        perm = [(source, index * replicas + rep) for source, (index, rep) in pairs]
        return lax.ppermute(array, ("dp", "rep"), perm)

    to_above = lambda index, rep: (along_y(index, 1), rep)
    to_below = lambda index, rep: (along_y(index, -1), rep)
    to_across = lambda index, rep: (across_x(index, rep % 2), rep)
    up = up_factor_matrix[0]
    up_y = swap(up, lambda index, rep: (along_y(index, 1 if rep % 2 else -1), rep))
    up_x = swap(up, to_across)
    up_other_y = swap(up_y, lambda index, rep: (index, rep ^ 1))
    message, first_tile = attention(
        latent_query_rows,
        rotary_query_parts,
        latent_cache_rows,
        rotary_cache_keys,
        lengths,
        adapters,
        output_weight,
    )
    gathered = exchange(message)
    gathered = gathered.reshape(-1, gathered.shape[-1])
    low, ids, own, *others = project(
        gathered, first_tile, value_up_weight, down_factor_matrix, output_weight
    )
    received = [
        swap(part, partner)
        for part, partner in zip(others, (to_above, to_across, to_below), strict=True)
    ]
    low = exchange(low)
    total, *parts = adapt(low, ids, own, received, (up, up_y, up_other_y, up_x))
    total = total.astype(F32)
    for part, bits in zip(parts, PEERS, strict=True):
        part = lax.ppermute(part, "dp", [(i, i ^ bits) for i in range(GROUPS)])
        total = total + part.astype(F32)
    return total.astype(BF16)


def solution(mesh):
    placed = (
        P(("rep", "dp"), None, None),
        P(("rep", "dp"), None),
        P(("rep", "dp"), None, None),
        P(("rep", "dp"), None, None),
        P(("rep", "dp")),
        P(("rep", "dp")),
        P("dp", None, None),
        P("dp", None),
        P("dp", None),
        P("dp", None, None),
    )
    return jax.shard_map(
        on_device, mesh=mesh, in_specs=placed, out_specs=P(("rep", "dp"), None), check_vma=False
    )
```

time: 61.4 us -> 58.9 us (0.959); the launches traced: 61.2 us -> 57.9 us
  blocking collectives: 28.1 us -> 10.2 us
  starting transfers between devices: 10.9 us -> 20.1 us
  waiting for transfers between devices: 9.92 us -> 15.8 us
  Pallas kernels: 11.4 us -> 10.2 us
  local copies, waits for them, and re-layouts: 0.01 us -> 0.81 us
    all_to_all x1 -> x0, blocking collectives: 16.7 us -> none  [on_device(): exchange(partial.reshape(GROUPS // 2, -1, partial.shape[-1]), axis_index_...]
    ppermute x3 -> x9, starting transfers between devices: 3.85 us -> 15.5 us  [the longest x6 8.89 us: swap(): return lax.ppermute(array, ('dp', 'rep'), perm)]
    ppermute x3 -> x9, waiting for transfers between devices: 0.01 us -> 5.92 us  [the longest x3 5.34 us: on_device(): part = lax.ppermute(part, 'dp', [(i, i ^ bits) for i in range(GROUPS)])]
    all_to_all x1, starting transfers between devices: 7.04 us -> 4.59 us  [on_device(): gathered = exchange(message)]
    all_to_all x1, blocking collectives: 11.4 us -> 10.2 us  [on_device(): low = exchange(low)]
    pallas_call x1, Pallas kernels: 4.94 us -> 4.09 us  [attention(): pl.pallas_call(attention_kernel, grid=(req_local // per_step,), in_specs=...]
    unnamed x2, local copies, waits for them, and re-layouts: 0.01 us -> 0.81 us
    reduce_sum x1 -> x0, other arithmetic: 0.78 us -> none  [on_device(): return jnp.sum(parts.astype(F32), axis=0).astype(BF16)]
  transfers between devices with their start and end apart: 4 -> 10, of which waited for: 1 -> 5; matrix products, arithmetic and copies ran while one was open for 0% -> 0% of each run, Pallas kernels for 7% -> 13%
where the time goes in v3:
time: 58.9 us; the launch traced here: 57.9 us
  starting transfers between devices  20.1 us (34%)
  waiting for transfers between devices  15.8 us (27%)
  Pallas kernels  10.2 us (17%)
  blocking collectives  10.2 us (17%)
  local copies, waits for them, and re-layouts  0.81 us (1%)
  other arithmetic  0.71 us (1%)
    all_to_all x1, blocking collectives, on_device(): low = exchange(low)  10.2 us
    all_to_all x1, waiting for transfers between devices, on_device(): gathered = exchange(message)  9.85 us
    ppermute x6, starting transfers between devices, swap(): return lax.ppermute(array, ('dp', 'rep'), perm)  8.89 us
    ppermute x3, starting transfers between devices, on_device(): part = lax.ppermute(part, 'dp', [(i, i ^ bits) for i in range(GROUPS)])  6.58 us
    ppermute x3, waiting for transfers between devices, on_device(): part = lax.ppermute(part, 'dp', [(i, i ^ bits) for i in range(GROUPS)])  5.34 us
    all_to_all x1, starting transfers between devices, on_device(): gathered = exchange(message)  4.59 us
    pallas_call x1, Pallas kernels, attention(): pl.pallas_call(attention_kernel, grid=(req_local // per_step,), in_specs=...  4.09 us
    pallas_call x1, Pallas kernels, project(): pl.pallas_call(project_kernel, in_specs=[in_vmem] * 2 + [pl.BlockSpec(mem...  3.58 us
  transfers between devices with their start and end apart: 10, of which 5 were waited for; matrix products, arithmetic and copies ran while one was open for 0% of the time, Pallas kernels for 13%

profile of v3, /device:TPU:160, one launch (start us, length us, event | category | flops | bytes accessed | tf_op | source)
XLA Modules:
  0.0 57.9 jit_solution(4635090159501133494)
XLA Ops:
  0.0 3.0 %collective-permute-start.3 = (bf16[64,7168]{1,0:T(8,128)(2,1)}, bf16[64,7168]{1,0:T(8,128)(2,1)S(1)}, u32[]{:S(2)}, u32[]{:S(2)}) collective-permute-start(bf16[64,7168]{1,0:T(8,128)(2,1)} %bitcast.3), channel_id=1, source_target_pairs={{0,192},{1,65},{2,194},{3,67},{4,196},{5,69},{6,198},{7,71},{8,200... | collective-permute-start | bytes 2752520 | tf_op jit(solution)/shard_map/ppermute | solution.py:380
  3.0 4.1 %attention.1 = (bf16[16,8,2176]{2,1,0:T(8,128)(2,1)S(1)}, bf16[512,1792]{1,0:T(8,128)(2,1)S(1)}) custom-call(s32[8]{0:T(128)} %lengths_ref.1, s32[8]{0:T(128)} %adapters_ref.1, bf16[8,64,512]{2,1,0:T(8,128)(2,1)} %query_ref.1, bf16[8,4096]{1,0:T(8,128)(2,1)} %rotary_ref.1, bf16[8,256,512]{2,1,0:T(8,128)(2,1)} %cache_ref.1, bf16[8,64,256]{2,1,0:T(8,128)(2,1)} %keys_ref.1, ...), custom_call_target="tpu_custom_call" | custom-call | tf_op jit(solution)/shard_map/attention/pallas_call | solution.py:106
  7.1 0.8 %copy-done = bf16[16,8,2176]{2,1,0:T(8,128)(2,1)} copy-done((bf16[16,8,2176]{2,1,0:T(8,128)(2,1)}, bf16[16,8,2176]{2,1,0:T(8,128)(2,1)S(1)}, u32[]{:S(2)}) %copy-start) | copy-done | bytes 557080
  7.9 4.6 %all-to-all-start = ((bf16[16,8,2176]{2,1,0:T(8,128)(2,1)}), bf16[16,8,2176]{2,1,0:T(8,128)(2,1)S(1)}, u32[]{:S(2)}, u32[]{:S(2)}) async-start(bf16[16,8,2176]{2,1,0:T(8,128)(2,1)} %copy-done), calls=%async_computation | async-start | bytes 1114112 | tf_op jit(solution)/shard_map/all_to_all | solution.py:398
  12.5 1.9 %collective-permute-start.5 = (bf16[64,7168]{1,0:T(8,128)(2,1)}, bf16[64,7168]{1,0:T(8,128)(2,1)}, u32[]{:S(2)}, u32[]{:S(2)}) collective-permute-start(bf16[64,7168]{1,0:T(8,128)(2,1)} %bitcast.4), channel_id=1, source_target_pairs={{0,16},{1,49},{2,18},{3,51},{4,20},{5,53},{6,22},{7,55},{8,24},{9,... | collective-permute-start | bytes 2752520 | tf_op jit(solution)/shard_map/ppermute | solution.py:380
  14.5 0.6 collective-permute-done.3.refs_1_
  15.0 0.1 collective-permute-start.4
  15.1 9.9 %all-to-all-done = bf16[16,8,2176]{2,1,0:T(8,128)(2,1)S(1)} async-done(((bf16[16,8,2176]{2,1,0:T(8,128)(2,1)}), bf16[16,8,2176]{2,1,0:T(8,128)(2,1)S(1)}, u32[]{:S(2)}, u32[]{:S(2)}) %all-to-all-start) | async-done | bytes 557088 | tf_op jit(solution)/shard_map/all_to_all | solution.py:398
  25.0 3.6 %project.1 = (f32[16,4,128]{2,1,0:T(4,128)S(1)}, f32[8,128]{1,0:T(8,128)S(1)}, f32[32,7168]{1,0:T(8,128)S(1)}, bf16[32,7168]{1,0:T(8,128)(2,1)S(1)}, bf16[32,716...) custom-call(bf16[128,2176]{1,0:T(8,128)(2,1)S(1)} %bitcast.2, bf16[512,1792]{1,0:T(8,128)(2,1)S(1)} %get-tuple-element.18.first_tile, ...), custom_call_target="tpu_custom_call" | custom-call | tf_op jit(solution)/shard_map/project/pallas_call | solution.py:268
  28.6 0.1 collective-permute-start
  28.6 0.7 %collective-permute-start.1 = (bf16[32,7168]{1,0:T(8,128)(2,1)S(1)}, bf16[32,7168]{1,0:T(8,128)(2,1)S(1)}, u32[]{:S(2)}, u32[]{:S(2)}) collective-permute-start(bf16[32,7168]{1,0:T(8,128)(2,1)S(1)} %get-tuple-element.23), channel_id=1, source_target_pairs={{0,16},{1,49},{2,18},{3,51},{4,20},{5,53},{6,22},{7,55},{8,24},{9,... | collective-permute-start | bytes 1376264 | tf_op jit(solution)/shard_map/ppermute | solution.py:380
  29.3 3.1 %collective-permute-start.2 = (bf16[32,7168]{1,0:T(8,128)(2,1)S(1)}, bf16[32,7168]{1,0:T(8,128)(2,1)S(1)}, u32[]{:S(2)}, u32[]{:S(2)}) collective-permute-start(bf16[32,7168]{1,0:T(8,128)(2,1)S(1)} %get-tuple-element.24), channel_id=1, source_target_pairs={{0,192},{1,193},{2,194},{3,195},{4,196},{5,197},{6,198},{7,199},{8... | collective-permute-start | bytes 1376264 | tf_op jit(solution)/shard_map/ppermute | solution.py:380
  32.4 10.2 %all_to_all.10.low_ref = f32[16,4,128]{2,1,0:T(4,128)S(1)} all-to-all(f32[16,4,128]{2,1,0:T(4,128)S(1)} %get-tuple-element.19), channel_id=1, replica_groups=mesh['dp'=16,'rep'=16] {'dp'}, dimensions={0} | all-to-all | bytes 65536 | tf_op jit(solution)/shard_map/all_to_all | solution.py:407
  42.7 0.0 collective-permute-done.5.refs_3_
  42.7 0.0 collective-permute-done.above_ref
  42.7 0.0 collective-permute-done.1.across_ref
  42.7 2.5 %adapt.1 = (bf16[8,7168]{1,0:T(8,128)(2,1)S(1)}, bf16[8,7168]{1,0:T(8,128)(2,1)S(1)}, bf16[8,7168]{1,0:T(8,128)(2,1)S(1)}, bf16[8,7168]{1,0:T(8,128)(2,1)S(1)}) custom-call(f32[16,4,128]{2,1,0:T(4,128)S(1)} %all_to_all.10.low_ref, f32[8,128]{1,0:T(8,128)S(1)} %get-tuple-element.20.ids_ref, f32[32,7168]{1,0:T(8,128)S(1)} %get-tuple-element.21.own_ref, ...), custom_call_target="tpu_custom_call" | custom-call | tf_op jit(solution)/shard_map/adapt/pallas_call | solution.py:341
  45.2 1.3 %collective-permute-start.6 = (bf16[8,7168]{1,0:T(8,128)(2,1)S(1)}, bf16[8,7168]{1,0:T(8,128)(2,1)S(1)}, u32[]{:S(2)}, u32[]{:S(2)}) collective-permute-start(bf16[8,7168]{1,0:T(8,128)(2,1)S(1)} %get-tuple-element.26), channel_id=1, source_target_pairs={{0,32},{16,48},{32,0},{48,16},{64,96},{80,112},{96,64},{112,80},{1... | collective-permute-start | bytes 344072 | tf_op jit(solution)/shard_map/ppermute | solution.py:411
  46.6 2.2 %collective-permute-start.7 = (bf16[8,7168]{1,0:T(8,128)(2,1)S(1)}, bf16[8,7168]{1,0:T(8,128)(2,1)S(1)}, u32[]{:S(2)}, u32[]{:S(2)}) collective-permute-start(bf16[8,7168]{1,0:T(8,128)(2,1)S(1)} %get-tuple-element.27), channel_id=1, source_target_pairs={{0,144},{16,128},{32,176},{48,160},{64,208},{80,192},{96,240},{112... | collective-permute-start | bytes 344072 | tf_op jit(solution)/shard_map/ppermute | solution.py:411
  48.8 3.1 %collective-permute-start.8 = (bf16[8,7168]{1,0:T(8,128)(2,1)S(1)}, bf16[8,7168]{1,0:T(8,128)(2,1)S(1)}, u32[]{:S(2)}, u32[]{:S(2)}) collective-permute-start(bf16[8,7168]{1,0:T(8,128)(2,1)S(1)} %get-tuple-element.28), channel_id=1, source_target_pairs={{0,176},{16,160},{32,144},{48,128},{64,240},{80,224},{96,208},{112... | collective-permute-start | bytes 344072 | tf_op jit(solution)/shard_map/ppermute | solution.py:411
  51.8 0.3 collective-permute-done.6
  52.2 1.7 %collective-permute-done.7 = bf16[8,7168]{1,0:T(8,128)(2,1)S(1)} collective-permute-done((bf16[8,7168]{1,0:T(8,128)(2,1)S(1)}, bf16[8,7168]{1,0:T(8,128)(2,1)S(1)}, u32[]{:S(2)}, u32[]{:S(2)}) %collective-permute-start.7) | collective-permute-done | bytes 114720 | tf_op jit(solution)/shard_map/ppermute | solution.py:411
  53.9 3.3 %collective-permute-done.8 = bf16[8,7168]{1,0:T(8,128)(2,1)S(1)} collective-permute-done((bf16[8,7168]{1,0:T(8,128)(2,1)S(1)}, bf16[8,7168]{1,0:T(8,128)(2,1)S(1)}, u32[]{:S(2)}, u32[]{:S(2)}) %collective-permute-start.8) | collective-permute-done | bytes 114720 | tf_op jit(solution)/shard_map/ppermute | solution.py:411
  57.2 0.7 %add_convert_fusion = bf16[8,7168]{1,0:T(8,128)(2,1)} fusion(bf16[8,7168]{1,0:T(8,128)(2,1)S(1)} %collective-permute-done.8, bf16[8,7168]{1,0:T(8,128)(2,1)S(1)} %collective-permute-done.7, bf16[8,7168]{1,0:T(8,128)(2,1)S(1)} %collective-permute-done.6, bf16[8,7168]{1,0:T(8,128)(2,1)S(1)} %get-tuple-element.25), kind=kLoop, calls=%fused_computation | loop fusion | flops 458752 | bytes 573440 | tf_op jit(solution)/shard_map/convert_element_type | solution.py:413
  (3 shorter events, 0.0 us)
Async XLA Ops:
  0.0 15.0 %collective-permute-start.3 = (bf16[64,7168]{1,0:T(8,128)(2,1)}, bf16[64,7168]{1,0:T(8,128)(2,1)S(1)}, u32[]{:S(2)}, u32[]{:S(2)}) collective-permute-start(bf16[64,7168]{1,0:T(8,128)(2,1)} %bitcast.3), channel_id=1, source_target_pairs={{0,192},{1,65},{2,194},{3,67},{4,196},{5,69},{6,198},{7,71},{8,200... | collective-permute-start | bytes 2752520 | tf_op jit(solution)/shard_map/ppermute | solution.py:380
  7.1 0.8 %copy-start = (bf16[16,8,2176]{2,1,0:T(8,128)(2,1)}, bf16[16,8,2176]{2,1,0:T(8,128)(2,1)S(1)}, u32[]{:S(2)}) copy-start(bf16[16,8,2176]{2,1,0:T(8,128)(2,1)S(1)} %get-tuple-element.17) | copy-start | bytes 1671172
  7.9 17.0 %all-to-all-start = ((bf16[16,8,2176]{2,1,0:T(8,128)(2,1)}), bf16[16,8,2176]{2,1,0:T(8,128)(2,1)S(1)}, u32[]{:S(2)}, u32[]{:S(2)}) async-start(bf16[16,8,2176]{2,1,0:T(8,128)(2,1)} %copy-done), calls=%async_computation | async-start | bytes 1114112 | tf_op jit(solution)/shard_map/all_to_all | solution.py:398
  12.5 30.1 %collective-permute-start.5 = (bf16[64,7168]{1,0:T(8,128)(2,1)}, bf16[64,7168]{1,0:T(8,128)(2,1)}, u32[]{:S(2)}, u32[]{:S(2)}) collective-permute-start(bf16[64,7168]{1,0:T(8,128)(2,1)} %bitcast.4), channel_id=1, source_target_pairs={{0,16},{1,49},{2,18},{3,51},{4,20},{5,53},{6,22},{7,55},{8,24},{9,... | collective-permute-start | bytes 2752520 | tf_op jit(solution)/shard_map/ppermute | solution.py:380
  15.0 27.7 %collective-permute-start.4 = (bf16[64,7168]{1,0:T(8,128)(2,1)S(1)}, bf16[64,7168]{1,0:T(8,128)(2,1)}, u32[]{:S(2)}, u32[]{:S(2)}) collective-permute-start(bf16[64,7168]{1,0:T(8,128)(2,1)S(1)} %collective-permute-done.3.refs_1_), channel_id=1, source_target_pairs={{0,1},{1,0},{2,3},{3,2},{4,5},{5,4},{6,7},{7,6},{8,9},{9,8},{10,11... | collective-permute-start | bytes 2752520 | tf_op jit(solution)/shard_map/ppermute | solution.py:380
  28.6 14.1 %collective-permute-start = (bf16[32,7168]{1,0:T(8,128)(2,1)S(1)}, bf16[32,7168]{1,0:T(8,128)(2,1)S(1)}, u32[]{:S(2)}, u32[]{:S(2)}) collective-permute-start(bf16[32,7168]{1,0:T(8,128)(2,1)S(1)} %get-tuple-element.22), channel_id=1, source_target_pairs={{0,64},{1,65},{2,66},{3,67},{4,68},{5,69},{6,70},{7,71},{8,72},{9,... | collective-permute-start | bytes 1376264 | tf_op jit(solution)/shard_map/ppermute | solution.py:380
  28.6 14.0 %collective-permute-start.1 = (bf16[32,7168]{1,0:T(8,128)(2,1)S(1)}, bf16[32,7168]{1,0:T(8,128)(2,1)S(1)}, u32[]{:S(2)}, u32[]{:S(2)}) collective-permute-start(bf16[32,7168]{1,0:T(8,128)(2,1)S(1)} %get-tuple-element.23), channel_id=1, source_target_pairs={{0,16},{1,49},{2,18},{3,51},{4,20},{5,53},{6,22},{7,55},{8,24},{9,... | collective-permute-start | bytes 1376264 | tf_op jit(solution)/shard_map/ppermute | solution.py:380
  29.3 13.4 %collective-permute-start.2 = (bf16[32,7168]{1,0:T(8,128)(2,1)S(1)}, bf16[32,7168]{1,0:T(8,128)(2,1)S(1)}, u32[]{:S(2)}, u32[]{:S(2)}) collective-permute-start(bf16[32,7168]{1,0:T(8,128)(2,1)S(1)} %get-tuple-element.24), channel_id=1, source_target_pairs={{0,192},{1,193},{2,194},{3,195},{4,196},{5,197},{6,198},{7,199},{8... | collective-permute-start | bytes 1376264 | tf_op jit(solution)/shard_map/ppermute | solution.py:380
  45.2 6.9 %collective-permute-start.6 = (bf16[8,7168]{1,0:T(8,128)(2,1)S(1)}, bf16[8,7168]{1,0:T(8,128)(2,1)S(1)}, u32[]{:S(2)}, u32[]{:S(2)}) collective-permute-start(bf16[8,7168]{1,0:T(8,128)(2,1)S(1)} %get-tuple-element.26), channel_id=1, source_target_pairs={{0,32},{16,48},{32,0},{48,16},{64,96},{80,112},{96,64},{112,80},{1... | collective-permute-start | bytes 344072 | tf_op jit(solution)/shard_map/ppermute | solution.py:411
  46.6 7.3 %collective-permute-start.7 = (bf16[8,7168]{1,0:T(8,128)(2,1)S(1)}, bf16[8,7168]{1,0:T(8,128)(2,1)S(1)}, u32[]{:S(2)}, u32[]{:S(2)}) collective-permute-start(bf16[8,7168]{1,0:T(8,128)(2,1)S(1)} %get-tuple-element.27), channel_id=1, source_target_pairs={{0,144},{16,128},{32,176},{48,160},{64,208},{80,192},{96,240},{112... | collective-permute-start | bytes 344072 | tf_op jit(solution)/shard_map/ppermute | solution.py:411
  48.8 8.4 %collective-permute-start.8 = (bf16[8,7168]{1,0:T(8,128)(2,1)S(1)}, bf16[8,7168]{1,0:T(8,128)(2,1)S(1)}, u32[]{:S(2)}, u32[]{:S(2)}) collective-permute-start(bf16[8,7168]{1,0:T(8,128)(2,1)S(1)} %get-tuple-element.28), channel_id=1, source_target_pairs={{0,176},{16,160},{32,144},{48,128},{64,240},{80,224},{96,208},{112... | collective-permute-start | bytes 344072 | tf_op jit(solution)/shard_map/ppermute | solution.py:411

commit v4 on v3

--- a/solution.py
+++ b/solution.py
@@ -12,6 +12,7 @@
 LANES = 128
 PER_STEP = 4
 TILE = 1792
+WIDE = 3584
 GROUPS = 16
 SIDE = 4
 CLASSES = 4
@@ -138,7 +139,7 @@
 
 
 MEMBERS = [[i for i in range(GROUPS) if class_of(i) == which] for which in range(CLASSES)]
-PEERS = (2, 9, 11)
+PEERS = (9, 11, 2)
 
 
 def across_x(index, core):
@@ -179,8 +180,8 @@
     ids_ref,
     own_ref,
     above_ref,
+    below_ref,
     across_ref,
-    below_ref,
     up,
     down,
     weight,
@@ -237,7 +238,7 @@
         chosen = turned[class_of(index)]
         low_ref[index, 0:1, :] = chosen[index : index + 1]
         above, below = along_y(index, 1), along_y(index, -1)
-        pairs = ((above, below), (below, above), (across_x(index, 0), across_x(index, 1)))
+        pairs = ((below, above), (above, below), (across_x(index, 0), across_x(index, 1)))
         for slot, pair in enumerate(pairs):
             pair = [chosen[rank : rank + 1] for rank in pair]
             low_ref[index, slot + 1 : slot + 2, :] = jnp.where(core == 0, *pair)
@@ -248,7 +249,7 @@
     ids_ref[...] = own_ids
 
     ordered = jnp.concatenate(
-        [values[lax.rem(which_own + step, CLASSES)] for step in (1, 2, 3, 0)], axis=0
+        [values[lax.rem(which_own + step, CLASSES)] for step in (1, 3, 2, 0)], axis=0
     )
     for tile in range(tiles):
         if tile > 0:
@@ -256,7 +257,7 @@
         part = weight[tile - 1] if tile > 0 else first_tile[...]
         total = jnp.dot(ordered, part, preferred_element_type=F32)
         columns = pl.ds(tile * TILE, TILE)
-        for i, other_ref in enumerate((above_ref, across_ref, below_ref)):
+        for i, other_ref in enumerate((above_ref, below_ref, across_ref)):
             other_ref[:, columns] = total[i * own_rows : (i + 1) * own_rows].astype(BF16)
         own_ref[:, columns] = total[3 * own_rows :]
 
@@ -292,8 +293,8 @@
     ids_ref,
     own_ref,
     above_ref,
+    below_ref,
     across_ref,
-    below_ref,
     *refs,
 ):
     up_refs, out_refs, (ups, totals, arrived) = refs[:4], refs[4:8], refs[8:]
@@ -305,7 +306,7 @@
         for slot, up_ref in enumerate(up_refs):
             copies.append(
                 pltpu.make_async_copy(
-                    up_ref.at[:, tile * TILE : (tile + 1) * TILE],
+                    up_ref.at[:, tile * WIDE : (tile + 1) * WIDE],
                     ups.at[tile, pl.ds(slot * adapter_total, adapter_total)],
                     arrived.at[tile, slot],
                 )
@@ -321,15 +322,15 @@
     _, place = own_place()
     each = own_rows // CLASSES
     for tile in range(tiles):
-        columns = pl.ds(tile * TILE, TILE)
+        columns = pl.ds(tile * WIDE, WIDE)
         total = own_ref[:, columns]
-        for received_ref in (above_ref, across_ref, below_ref):
+        for received_ref in (above_ref, below_ref, across_ref):
             total = total + received_ref[:, columns].astype(F32)
         for copy in copies[4 * tile : 4 * tile + 4]:
             copy.wait()
         total = total + jnp.dot(chosen, ups[tile], preferred_element_type=F32)
-        totals[...] = total.reshape(CLASSES, each, TILE)
-        for turn, out_ref in enumerate(out_refs):
+        totals[...] = total.reshape(CLASSES, each, WIDE)
+        for turn, out_ref in zip((0, 2, 3, 1), out_refs, strict=True):
             out_ref[:, columns] = totals[place ^ turn].astype(BF16)
 
 
@@ -337,15 +338,15 @@
     in_vmem = pl.BlockSpec(memory_space=pltpu.VMEM)
     near = [pltpu.with_memory_space_constraint(a, pltpu.VMEM) for a in (own, *received)]
     rows, width = own.shape
-    tiles = width // TILE
+    tiles = width // WIDE
     return pl.pallas_call(
         adapt_kernel,
         in_specs=[in_vmem] * 6 + [pl.BlockSpec(memory_space=pl.ANY)] * 4,
         out_specs=[in_vmem] * 4,
         out_shape=[jax.ShapeDtypeStruct((rows // CLASSES, width), BF16)] * 4,
         scratch_shapes=[
-            pltpu.VMEM((tiles, 4 * ups[0].shape[0], TILE), BF16),
-            pltpu.VMEM((CLASSES, rows // CLASSES, TILE), F32),
+            pltpu.VMEM((tiles, 4 * ups[0].shape[0], WIDE), BF16),
+            pltpu.VMEM((CLASSES, rows // CLASSES, WIDE), F32),
             pltpu.SemaphoreType.DMA((tiles, 4)),
         ],
         compiler_params=pltpu.CompilerParams(vmem_limit_bytes=16 << 20),
@@ -383,7 +384,7 @@
     to_below = lambda index, rep: (along_y(index, -1), rep)
     to_across = lambda index, rep: (across_x(index, rep % 2), rep)
     up = up_factor_matrix[0]
-    up_y = swap(up, lambda index, rep: (along_y(index, 1 if rep % 2 else -1), rep))
+    up_y = swap(up, lambda index, rep: (along_y(index, -1 if rep % 2 else 1), rep))
     up_x = swap(up, to_across)
     up_other_y = swap(up_y, lambda index, rep: (index, rep ^ 1))
     message, first_tile = attention(
@@ -402,7 +403,7 @@
     )
     received = [
         swap(part, partner)
-        for part, partner in zip(others, (to_above, to_across, to_below), strict=True)
+        for part, partner in zip(others, (to_above, to_below, to_across), strict=True)
     ]
     low = exchange(low)
     total, *parts = adapt(low, ids, own, received, (up, up_y, up_other_y, up_x))

time: 58.9 us -> 56.6 us (0.961); the launches traced: 57.9 us -> 56.3 us
  waiting for transfers between devices: 15.8 us -> 13.1 us
  blocking collectives: 10.2 us -> 10.8 us
  starting transfers between devices: 20.1 us -> 20.7 us
    all_to_all x1, starting transfers between devices: 4.59 us -> 6.75 us  [on_device(): gathered = exchange(message)]
    ppermute x6, starting transfers between devices: 8.89 us -> 7.39 us  [swap(): return lax.ppermute(array, ('dp', 'rep'), perm)]
    ppermute x3, waiting for transfers between devices: 5.34 us -> 4.02 us  [on_device(): part = lax.ppermute(part, 'dp', [(i, i ^ bits) for i in range(GROUPS)])]
    all_to_all x1, waiting for transfers between devices: 9.85 us -> 9.09 us  [on_device(): gathered = exchange(message)]
  transfers between devices with their start and end apart: 10 -> 10, of which waited for: 5 -> 4; matrix products, arithmetic and copies ran while one was open for 0% -> 0% of each run, Pallas kernels for 13% -> 14%
where the time goes in v4:
time: 56.6 us; the launch traced here: 56.3 us
  starting transfers between devices  20.7 us (37%)
  waiting for transfers between devices  13.1 us (23%)
  blocking collectives  10.8 us (19%)
  Pallas kernels  10.1 us (18%)
  local copies, waits for them, and re-layouts  0.81 us (1%)
  other arithmetic  0.71 us (1%)
    all_to_all x1, blocking collectives, on_device(): low = exchange(low)  10.8 us
    all_to_all x1, waiting for transfers between devices, on_device(): gathered = exchange(message)  9.09 us
    ppermute x6, starting transfers between devices, swap(): return lax.ppermute(array, ('dp', 'rep'), perm)  7.39 us
    all_to_all x1, starting transfers between devices, on_device(): gathered = exchange(message)  6.75 us
    ppermute x3, starting transfers between devices, on_device(): part = lax.ppermute(part, 'dp', [(i, i ^ bits) for i in range(GROUPS)])  6.58 us
    pallas_call x1, Pallas kernels, attention(): pl.pallas_call(attention_kernel, grid=(req_local // per_step,), in_specs=...  4.09 us
    ppermute x3, waiting for transfers between devices, on_device(): part = lax.ppermute(part, 'dp', [(i, i ^ bits) for i in range(GROUPS)])  4.02 us
    pallas_call x1, Pallas kernels, project(): pl.pallas_call(project_kernel, in_specs=[in_vmem] * 2 + [pl.BlockSpec(mem...  3.58 us
  transfers between devices with their start and end apart: 10, of which 4 were waited for; matrix products, arithmetic and copies ran while one was open for 0% of the time, Pallas kernels for 14%

profile of v4, /device:TPU:160, one launch (start us, length us, event | category | flops | bytes accessed | tf_op | source)
XLA Modules:
  0.0 56.3 jit_solution(1188079522321436955)
XLA Ops:
  0.0 1.6 %collective-permute-start.3 = (bf16[64,7168]{1,0:T(8,128)(2,1)}, bf16[64,7168]{1,0:T(8,128)(2,1)S(1)}, u32[]{:S(2)}, u32[]{:S(2)}) collective-permute-start(bf16[64,7168]{1,0:T(8,128)(2,1)} %bitcast.3), channel_id=1, source_target_pairs={{0,64},{1,193},{2,66},{3,195},{4,68},{5,197},{6,70},{7,199},{8,72}... | collective-permute-start | bytes 2752520 | tf_op jit(solution)/shard_map/ppermute | solution.py:381
  1.6 4.1 %attention.1 = (bf16[16,8,2176]{2,1,0:T(8,128)(2,1)S(1)}, bf16[512,1792]{1,0:T(8,128)(2,1)S(1)}) custom-call(s32[8]{0:T(128)} %lengths_ref.1, s32[8]{0:T(128)} %adapters_ref.1, bf16[8,64,512]{2,1,0:T(8,128)(2,1)} %query_ref.1, bf16[8,4096]{1,0:T(8,128)(2,1)} %rotary_ref.1, bf16[8,256,512]{2,1,0:T(8,128)(2,1)} %cache_ref.1, bf16[8,64,256]{2,1,0:T(8,128)(2,1)} %keys_ref.1, ...), custom_call_target="tpu_custom_call" | custom-call | tf_op jit(solution)/shard_map/attention/pallas_call | solution.py:107
  5.7 0.8 %copy-done = bf16[16,8,2176]{2,1,0:T(8,128)(2,1)} copy-done((bf16[16,8,2176]{2,1,0:T(8,128)(2,1)}, bf16[16,8,2176]{2,1,0:T(8,128)(2,1)S(1)}, u32[]{:S(2)}) %copy-start) | copy-done | bytes 557080
  6.5 6.8 %all-to-all-start = ((bf16[16,8,2176]{2,1,0:T(8,128)(2,1)}), bf16[16,8,2176]{2,1,0:T(8,128)(2,1)S(1)}, u32[]{:S(2)}, u32[]{:S(2)}) async-start(bf16[16,8,2176]{2,1,0:T(8,128)(2,1)} %copy-done), calls=%async_computation | async-start | bytes 1114112 | tf_op jit(solution)/shard_map/all_to_all | solution.py:399
  13.3 1.9 %collective-permute-start.5 = (bf16[64,7168]{1,0:T(8,128)(2,1)}, bf16[64,7168]{1,0:T(8,128)(2,1)}, u32[]{:S(2)}, u32[]{:S(2)}) collective-permute-start(bf16[64,7168]{1,0:T(8,128)(2,1)} %bitcast.4), channel_id=1, source_target_pairs={{0,16},{1,49},{2,18},{3,51},{4,20},{5,53},{6,22},{7,55},{8,24},{9,... | collective-permute-start | bytes 2752520 | tf_op jit(solution)/shard_map/ppermute | solution.py:381
  15.2 0.0 collective-permute-done.3.refs_1_
  15.2 0.0 collective-permute-start.4
  15.2 9.1 %all-to-all-done = bf16[16,8,2176]{2,1,0:T(8,128)(2,1)S(1)} async-done(((bf16[16,8,2176]{2,1,0:T(8,128)(2,1)}), bf16[16,8,2176]{2,1,0:T(8,128)(2,1)S(1)}, u32[]{:S(2)}, u32[]{:S(2)}) %all-to-all-start) | async-done | bytes 557088 | tf_op jit(solution)/shard_map/all_to_all | solution.py:399
  24.3 3.6 %project.1 = (f32[16,4,128]{2,1,0:T(4,128)S(1)}, f32[8,128]{1,0:T(8,128)S(1)}, f32[32,7168]{1,0:T(8,128)S(1)}, bf16[32,7168]{1,0:T(8,128)(2,1)S(1)}, bf16[32,716...) custom-call(bf16[128,2176]{1,0:T(8,128)(2,1)S(1)} %bitcast.2, bf16[512,1792]{1,0:T(8,128)(2,1)S(1)} %get-tuple-element.18.first_tile, ...), custom_call_target="tpu_custom_call" | custom-call | tf_op jit(solution)/shard_map/project/pallas_call | solution.py:269
  27.9 0.5 collective-permute-start
  28.3 2.8 %collective-permute-start.1 = (bf16[32,7168]{1,0:T(8,128)(2,1)S(1)}, bf16[32,7168]{1,0:T(8,128)(2,1)S(1)}, u32[]{:S(2)}, u32[]{:S(2)}) collective-permute-start(bf16[32,7168]{1,0:T(8,128)(2,1)S(1)} %get-tuple-element.23), channel_id=1, source_target_pairs={{0,192},{1,193},{2,194},{3,195},{4,196},{5,197},{6,198},{7,199},{8... | collective-permute-start | bytes 1376264 | tf_op jit(solution)/shard_map/ppermute | solution.py:381
  31.2 0.6 %collective-permute-start.2 = (bf16[32,7168]{1,0:T(8,128)(2,1)S(1)}, bf16[32,7168]{1,0:T(8,128)(2,1)S(1)}, u32[]{:S(2)}, u32[]{:S(2)}) collective-permute-start(bf16[32,7168]{1,0:T(8,128)(2,1)S(1)} %get-tuple-element.24), channel_id=1, source_target_pairs={{0,16},{1,49},{2,18},{3,51},{4,20},{5,53},{6,22},{7,55},{8,24},{9,... | collective-permute-start | bytes 1376264 | tf_op jit(solution)/shard_map/ppermute | solution.py:381
  31.7 10.8 %all_to_all.10.low_ref = f32[16,4,128]{2,1,0:T(4,128)S(1)} all-to-all(f32[16,4,128]{2,1,0:T(4,128)S(1)} %get-tuple-element.19), channel_id=1, replica_groups=mesh['dp'=16,'rep'=16] {'dp'}, dimensions={0} | all-to-all | bytes 65536 | tf_op jit(solution)/shard_map/all_to_all | solution.py:408
  42.6 0.0 collective-permute-done.above_ref
  42.6 0.0 collective-permute-done.1.below_ref
  42.6 0.0 collective-permute-done.2.across_ref
  42.6 2.4 %adapt.1 = (bf16[8,7168]{1,0:T(8,128)(2,1)S(1)}, bf16[8,7168]{1,0:T(8,128)(2,1)S(1)}, bf16[8,7168]{1,0:T(8,128)(2,1)S(1)}, bf16[8,7168]{1,0:T(8,128)(2,1)S(1)}) custom-call(f32[16,4,128]{2,1,0:T(4,128)S(1)} %all_to_all.10.low_ref, f32[8,128]{1,0:T(8,128)S(1)} %get-tuple-element.20.ids_ref, f32[32,7168]{1,0:T(8,128)S(1)} %get-tuple-element.21.own_ref, ...), custom_call_target="tpu_custom_call" | custom-call | tf_op jit(solution)/shard_map/adapt/pallas_call | solution.py:342
  45.0 1.3 %collective-permute-start.6 = (bf16[8,7168]{1,0:T(8,128)(2,1)S(1)}, bf16[8,7168]{1,0:T(8,128)(2,1)S(1)}, u32[]{:S(2)}, u32[]{:S(2)}) collective-permute-start(bf16[8,7168]{1,0:T(8,128)(2,1)S(1)} %get-tuple-element.26), channel_id=1, source_target_pairs={{0,144},{16,128},{32,176},{48,160},{64,208},{80,192},{96,240},{112... | collective-permute-start | bytes 344072 | tf_op jit(solution)/shard_map/ppermute | solution.py:412
  46.3 3.0 %collective-permute-start.7 = (bf16[8,7168]{1,0:T(8,128)(2,1)S(1)}, bf16[8,7168]{1,0:T(8,128)(2,1)S(1)}, u32[]{:S(2)}, u32[]{:S(2)}) collective-permute-start(bf16[8,7168]{1,0:T(8,128)(2,1)S(1)} %get-tuple-element.27), channel_id=1, source_target_pairs={{0,176},{16,160},{32,144},{48,128},{64,240},{80,224},{96,208},{112... | collective-permute-start | bytes 344072 | tf_op jit(solution)/shard_map/ppermute | solution.py:412
  49.3 2.3 %collective-permute-start.8 = (bf16[8,7168]{1,0:T(8,128)(2,1)S(1)}, bf16[8,7168]{1,0:T(8,128)(2,1)S(1)}, u32[]{:S(2)}, u32[]{:S(2)}) collective-permute-start(bf16[8,7168]{1,0:T(8,128)(2,1)S(1)} %get-tuple-element.28), channel_id=1, source_target_pairs={{0,32},{16,48},{32,0},{48,16},{64,96},{80,112},{96,64},{112,80},{1... | collective-permute-start | bytes 344072 | tf_op jit(solution)/shard_map/ppermute | solution.py:412
  51.6 0.7 %collective-permute-done.6 = bf16[8,7168]{1,0:T(8,128)(2,1)S(1)} collective-permute-done((bf16[8,7168]{1,0:T(8,128)(2,1)S(1)}, bf16[8,7168]{1,0:T(8,128)(2,1)S(1)}, u32[]{:S(2)}, u32[]{:S(2)}) %collective-permute-start.6) | collective-permute-done | bytes 114720 | tf_op jit(solution)/shard_map/ppermute | solution.py:412
  52.3 2.4 %collective-permute-done.7 = bf16[8,7168]{1,0:T(8,128)(2,1)S(1)} collective-permute-done((bf16[8,7168]{1,0:T(8,128)(2,1)S(1)}, bf16[8,7168]{1,0:T(8,128)(2,1)S(1)}, u32[]{:S(2)}, u32[]{:S(2)}) %collective-permute-start.7) | collective-permute-done | bytes 114720 | tf_op jit(solution)/shard_map/ppermute | solution.py:412
  54.7 0.9 %collective-permute-done.8 = bf16[8,7168]{1,0:T(8,128)(2,1)S(1)} collective-permute-done((bf16[8,7168]{1,0:T(8,128)(2,1)S(1)}, bf16[8,7168]{1,0:T(8,128)(2,1)S(1)}, u32[]{:S(2)}, u32[]{:S(2)}) %collective-permute-start.8) | collective-permute-done | bytes 114720 | tf_op jit(solution)/shard_map/ppermute | solution.py:412
  55.6 0.7 %add_convert_fusion = bf16[8,7168]{1,0:T(8,128)(2,1)} fusion(bf16[8,7168]{1,0:T(8,128)(2,1)S(1)} %collective-permute-done.8, bf16[8,7168]{1,0:T(8,128)(2,1)S(1)} %collective-permute-done.7, bf16[8,7168]{1,0:T(8,128)(2,1)S(1)} %collective-permute-done.6, bf16[8,7168]{1,0:T(8,128)(2,1)S(1)} %get-tuple-element.25), kind=kLoop, calls=%fused_computation | loop fusion | flops 458752 | bytes 573440 | tf_op jit(solution)/shard_map/convert_element_type | solution.py:414
  (3 shorter events, 0.0 us)
Async XLA Ops:
  0.0 15.2 %collective-permute-start.3 = (bf16[64,7168]{1,0:T(8,128)(2,1)}, bf16[64,7168]{1,0:T(8,128)(2,1)S(1)}, u32[]{:S(2)}, u32[]{:S(2)}) collective-permute-start(bf16[64,7168]{1,0:T(8,128)(2,1)} %bitcast.3), channel_id=1, source_target_pairs={{0,64},{1,193},{2,66},{3,195},{4,68},{5,197},{6,70},{7,199},{8,72}... | collective-permute-start | bytes 2752520 | tf_op jit(solution)/shard_map/ppermute | solution.py:381
  5.7 0.8 %copy-start = (bf16[16,8,2176]{2,1,0:T(8,128)(2,1)}, bf16[16,8,2176]{2,1,0:T(8,128)(2,1)S(1)}, u32[]{:S(2)}) copy-start(bf16[16,8,2176]{2,1,0:T(8,128)(2,1)S(1)} %get-tuple-element.17) | copy-start | bytes 1671172
  6.5 17.8 %all-to-all-start = ((bf16[16,8,2176]{2,1,0:T(8,128)(2,1)}), bf16[16,8,2176]{2,1,0:T(8,128)(2,1)S(1)}, u32[]{:S(2)}, u32[]{:S(2)}) async-start(bf16[16,8,2176]{2,1,0:T(8,128)(2,1)} %copy-done), calls=%async_computation | async-start | bytes 1114112 | tf_op jit(solution)/shard_map/all_to_all | solution.py:399
  13.3 29.3 %collective-permute-start.5 = (bf16[64,7168]{1,0:T(8,128)(2,1)}, bf16[64,7168]{1,0:T(8,128)(2,1)}, u32[]{:S(2)}, u32[]{:S(2)}) collective-permute-start(bf16[64,7168]{1,0:T(8,128)(2,1)} %bitcast.4), channel_id=1, source_target_pairs={{0,16},{1,49},{2,18},{3,51},{4,20},{5,53},{6,22},{7,55},{8,24},{9,... | collective-permute-start | bytes 2752520 | tf_op jit(solution)/shard_map/ppermute | solution.py:381
  15.2 27.4 %collective-permute-start.4 = (bf16[64,7168]{1,0:T(8,128)(2,1)S(1)}, bf16[64,7168]{1,0:T(8,128)(2,1)}, u32[]{:S(2)}, u32[]{:S(2)}) collective-permute-start(bf16[64,7168]{1,0:T(8,128)(2,1)S(1)} %collective-permute-done.3.refs_1_), channel_id=1, source_target_pairs={{0,1},{1,0},{2,3},{3,2},{4,5},{5,4},{6,7},{7,6},{8,9},{9,8},{10,11... | collective-permute-start | bytes 2752520 | tf_op jit(solution)/shard_map/ppermute | solution.py:381
  27.9 14.7 %collective-permute-start = (bf16[32,7168]{1,0:T(8,128)(2,1)S(1)}, bf16[32,7168]{1,0:T(8,128)(2,1)S(1)}, u32[]{:S(2)}, u32[]{:S(2)}) collective-permute-start(bf16[32,7168]{1,0:T(8,128)(2,1)S(1)} %get-tuple-element.22), channel_id=1, source_target_pairs={{0,64},{1,65},{2,66},{3,67},{4,68},{5,69},{6,70},{7,71},{8,72},{9,... | collective-permute-start | bytes 1376264 | tf_op jit(solution)/shard_map/ppermute | solution.py:381
  28.3 14.2 %collective-permute-start.1 = (bf16[32,7168]{1,0:T(8,128)(2,1)S(1)}, bf16[32,7168]{1,0:T(8,128)(2,1)S(1)}, u32[]{:S(2)}, u32[]{:S(2)}) collective-permute-start(bf16[32,7168]{1,0:T(8,128)(2,1)S(1)} %get-tuple-element.23), channel_id=1, source_target_pairs={{0,192},{1,193},{2,194},{3,195},{4,196},{5,197},{6,198},{7,199},{8... | collective-permute-start | bytes 1376264 | tf_op jit(solution)/shard_map/ppermute | solution.py:381
  31.2 11.4 %collective-permute-start.2 = (bf16[32,7168]{1,0:T(8,128)(2,1)S(1)}, bf16[32,7168]{1,0:T(8,128)(2,1)S(1)}, u32[]{:S(2)}, u32[]{:S(2)}) collective-permute-start(bf16[32,7168]{1,0:T(8,128)(2,1)S(1)} %get-tuple-element.24), channel_id=1, source_target_pairs={{0,16},{1,49},{2,18},{3,51},{4,20},{5,53},{6,22},{7,55},{8,24},{9,... | collective-permute-start | bytes 1376264 | tf_op jit(solution)/shard_map/ppermute | solution.py:381
  45.0 7.3 %collective-permute-start.6 = (bf16[8,7168]{1,0:T(8,128)(2,1)S(1)}, bf16[8,7168]{1,0:T(8,128)(2,1)S(1)}, u32[]{:S(2)}, u32[]{:S(2)}) collective-permute-start(bf16[8,7168]{1,0:T(8,128)(2,1)S(1)} %get-tuple-element.26), channel_id=1, source_target_pairs={{0,144},{16,128},{32,176},{48,160},{64,208},{80,192},{96,240},{112... | collective-permute-start | bytes 344072 | tf_op jit(solution)/shard_map/ppermute | solution.py:412
  46.3 8.4 %collective-permute-start.7 = (bf16[8,7168]{1,0:T(8,128)(2,1)S(1)}, bf16[8,7168]{1,0:T(8,128)(2,1)S(1)}, u32[]{:S(2)}, u32[]{:S(2)}) collective-permute-start(bf16[8,7168]{1,0:T(8,128)(2,1)S(1)} %get-tuple-element.27), channel_id=1, source_target_pairs={{0,176},{16,160},{32,144},{48,128},{64,240},{80,224},{96,208},{112... | collective-permute-start | bytes 344072 | tf_op jit(solution)/shard_map/ppermute | solution.py:412
  49.3 6.3 %collective-permute-start.8 = (bf16[8,7168]{1,0:T(8,128)(2,1)S(1)}, bf16[8,7168]{1,0:T(8,128)(2,1)S(1)}, u32[]{:S(2)}, u32[]{:S(2)}) collective-permute-start(bf16[8,7168]{1,0:T(8,128)(2,1)S(1)} %get-tuple-element.28), channel_id=1, source_target_pairs={{0,32},{16,48},{32,0},{48,16},{64,96},{80,112},{96,64},{112,80},{1... | collective-permute-start | bytes 344072 | tf_op jit(solution)/shard_map/ppermute | solution.py:412

commit v5 on v4

--- a/solution.py
+++ b/solution.py
@@ -11,7 +11,8 @@
 exponent_scale = 192.0 ** (-0.5) * math.log2(math.e)
 LANES = 128
 PER_STEP = 4
-TILE = 1792
+STAGED = 2816
+TILE = 2176
 WIDE = 3584
 GROUPS = 16
 SIDE = 4
@@ -31,14 +32,15 @@
     weight_out,
     rows,
     attended,
+    message,
     arrived,
 ):
-    staging = pltpu.make_async_copy(weight_in.at[:, :TILE], weight_out, arrived.at[0])
+    staging = pltpu.make_async_copy(weight_in.at[:, :STAGED], weight_out, arrived.at[0])
     req_local = rotary_ref.shape[0]
     heads = query_ref.shape[1]
     rope = keys_ref.shape[1]
     cache_len, latent = cache_ref.shape[1:]
-    groups = out_ref.shape[0]
+    groups = message.shape[0]
     per_group = heads // groups
     per_step = query_ref.shape[0]
     step = pl.program_id(0)
@@ -82,15 +84,25 @@
         for request in range(req_local):
             ids = jnp.where(row == request, adapters_ref[request], ids)
         ids = ids.astype(F32).astype(BF16)
+        leaving = []
         for group in range(groups):
             for own in range(per_group):
                 picked = pl.ds(group * per_group + own, req_local, stride=heads)
                 for part in range(latent // LANES):
                     column = own * latent + part * LANES
-                    out_ref[group, :, column : column + LANES] = attended[part, picked, :].astype(
+                    message[group, :, column : column + LANES] = attended[part, picked, :].astype(
                         BF16
                     )
-            out_ref[group, :, per_group * latent :] = ids
+            message[group, :, per_group * latent :] = ids
+            if (group + 1) % 4 == 0:
+                part = pl.ds(group - 3, 4)
+                sent = pltpu.make_async_copy(
+                    message.at[part], out_ref.at[part], arrived.at[1 + group // 4]
+                )
+                sent.start()
+                leaving.append(sent)
+        for sent in leaving:
+            sent.wait()
         staging.wait()
 
 
@@ -117,17 +129,18 @@
             anywhere,
         ],
         out_specs=[
-            pl.BlockSpec((GROUPS, req_local, width), lambda i: (0, 0, 0)),
             anywhere,
+            anywhere,
         ],
         out_shape=[
-            jax.ShapeDtypeStruct((GROUPS, req_local, width), BF16),
-            pltpu.VMEM((weight.shape[0], TILE), BF16),
+            pltpu.HBM((GROUPS, req_local, width), BF16),
+            pltpu.VMEM((weight.shape[0], STAGED), BF16),
         ],
         scratch_shapes=[
             pltpu.VMEM((req_local * heads, LANES), F32),
             pltpu.VMEM((latent // LANES, req_local * heads, LANES), F32),
-            pltpu.SemaphoreType.DMA((1,)),
+            pltpu.VMEM((GROUPS, req_local, width), BF16),
+            pltpu.SemaphoreType.DMA((5,)),
         ],
         compiler_params=pltpu.CompilerParams(vmem_limit_bytes=16 << 20),
         name="attention",
@@ -140,6 +153,7 @@
 
 MEMBERS = [[i for i in range(GROUPS) if class_of(i) == which] for which in range(CLASSES)]
 PEERS = (9, 11, 2)
+SENDING = ((1, 3, 2), (2, 1, 3))
 
 
 def across_x(index, core):
@@ -179,9 +193,9 @@
     low_ref,
     ids_ref,
     own_ref,
-    above_ref,
-    below_ref,
-    across_ref,
+    first_ref,
+    second_ref,
+    third_ref,
     up,
     down,
     weight,
@@ -194,7 +208,7 @@
         pltpu.make_async_copy(down_ref, down, arrived.at[1]),
     ] + [
         pltpu.make_async_copy(
-            weight_ref.at[:, tile * TILE : (tile + 1) * TILE],
+            weight_ref.at[:, STAGED + (tile - 1) * TILE : STAGED + tile * TILE],
             weight.at[tile - 1],
             arrived.at[1 + tile],
         )
@@ -248,16 +262,17 @@
         own_ids = jnp.where(which_own == which, pltpu.roll(ids, turns[which], 1), own_ids)
     ids_ref[...] = own_ids
 
+    steps = [jnp.where(core == 0, *pair) for pair in zip(*SENDING, strict=True)] + [0]
     ordered = jnp.concatenate(
-        [values[lax.rem(which_own + step, CLASSES)] for step in (1, 3, 2, 0)], axis=0
+        [values[lax.rem(which_own + step, CLASSES)] for step in steps], axis=0
     )
     for tile in range(tiles):
         if tile > 0:
             copies[1 + tile].wait()
         part = weight[tile - 1] if tile > 0 else first_tile[...]
         total = jnp.dot(ordered, part, preferred_element_type=F32)
-        columns = pl.ds(tile * TILE, TILE)
-        for i, other_ref in enumerate((above_ref, below_ref, across_ref)):
+        columns = pl.ds(0, STAGED) if tile == 0 else pl.ds(STAGED + (tile - 1) * TILE, TILE)
+        for i, other_ref in enumerate((first_ref, second_ref, third_ref)):
             other_ref[:, columns] = total[i * own_rows : (i + 1) * own_rows].astype(BF16)
         own_ref[:, columns] = total[3 * own_rows :]
 
@@ -265,7 +280,7 @@
 def project(gathered, first_tile, value_up, down, weight):
     in_vmem = pl.BlockSpec(memory_space=pltpu.VMEM)
     rows, (depth, width) = gathered.shape[0], weight.shape
-    tiles = width // TILE
+    tiles = 1 + (width - STAGED) // TILE
     return pl.pallas_call(
         project_kernel,
         in_specs=[in_vmem] * 2 + [pl.BlockSpec(memory_space=pl.ANY)] * 3,
@@ -292,9 +307,9 @@
     low_ref,
     ids_ref,
     own_ref,
-    above_ref,
-    below_ref,
-    across_ref,
+    first_ref,
+    second_ref,
+    third_ref,
     *refs,
 ):
     up_refs, out_refs, (ups, totals, arrived) = refs[:4], refs[4:8], refs[8:]
@@ -324,7 +339,7 @@
     for tile in range(tiles):
         columns = pl.ds(tile * WIDE, WIDE)
         total = own_ref[:, columns]
-        for received_ref in (above_ref, below_ref, across_ref):
+        for received_ref in (first_ref, second_ref, third_ref):
             total = total + received_ref[:, columns].astype(F32)
         for copy in copies[4 * tile : 4 * tile + 4]:
             copy.wait()
@@ -401,9 +416,10 @@
     low, ids, own, *others = project(
         gathered, first_tile, value_up_weight, down_factor_matrix, output_weight
     )
+    ways = {1: to_above, 2: to_across, 3: to_below}
     received = [
-        swap(part, partner)
-        for part, partner in zip(others, (to_above, to_below, to_across), strict=True)
+        swap(part, lambda index, rep, steps=steps: ways[steps[rep % 2]](index, rep))
+        for part, steps in zip(others, zip(*SENDING, strict=True), strict=True)
     ]
     low = exchange(low)
     total, *parts = adapt(low, ids, own, received, (up, up_y, up_other_y, up_x))

time: 56.6 us -> 56.3 us (level)
  local copies, waits for them, and re-layouts: 0.81 us -> 0 us
    unnamed x2 -> x0, local copies, waits for them, and re-layouts: 0.81 us -> none
    pallas_call x1, Pallas kernels: 4.09 us -> 4.76 us  [attention(): pl.pallas_call(attention_kernel, grid=(req_local // per_step,), in_specs=...]
where the time goes in v5:
time: 56.3 us; the launch traced here: 56 us
  starting transfers between devices  20.7 us (37%)
  waiting for transfers between devices  13.1 us (23%)
  blocking collectives  10.8 us (19%)
  Pallas kernels  10.6 us (19%)
  other arithmetic  0.71 us (1%)
    all_to_all x1, blocking collectives, on_device(): low = exchange(low)  10.8 us
    all_to_all x1, waiting for transfers between devices, on_device(): gathered = exchange(message)  9.09 us
    ppermute x6, starting transfers between devices, swap(): return lax.ppermute(array, ('dp', 'rep'), perm)  7.39 us
    all_to_all x1, starting transfers between devices, on_device(): gathered = exchange(message)  6.76 us
    ppermute x3, starting transfers between devices, on_device(): part = lax.ppermute(part, 'dp', [(i, i ^ bits) for i in range(GROUPS)])  6.58 us
    pallas_call x1, Pallas kernels, attention(): pl.pallas_call(attention_kernel, grid=(req_local // per_step,), in_specs=...  4.76 us
    ppermute x3, waiting for transfers between devices, on_device(): part = lax.ppermute(part, 'dp', [(i, i ^ bits) for i in range(GROUPS)])  4.02 us
    pallas_call x1, Pallas kernels, project(): pl.pallas_call(project_kernel, in_specs=[in_vmem] * 2 + [pl.BlockSpec(mem...  3.31 us
  transfers between devices with their start and end apart: 10, of which 4 were waited for; matrix products, arithmetic and copies ran while one was open for 0% of the time, Pallas kernels for 14%

profile of v5, /device:TPU:160, one launch (start us, length us, event | category | flops | bytes accessed | tf_op | source)
XLA Modules:
  0.0 56.0 jit_solution(330594694348019014)
XLA Ops:
  0.0 1.6 %collective-permute-start.3 = (bf16[64,7168]{1,0:T(8,128)(2,1)}, bf16[64,7168]{1,0:T(8,128)(2,1)}, u32[]{:S(2)}, u32[]{:S(2)}) collective-permute-start(bf16[64,7168]{1,0:T(8,128)(2,1)} %bitcast.3), channel_id=1, source_target_pairs={{0,64},{1,193},{2,66},{3,195},{4,68},{5,197},{6,70},{7,199},{8,72}... | collective-permute-start | bytes 2752520 | tf_op jit(solution)/shard_map/ppermute | solution.py:396
  1.6 4.8 %attention.1 = (bf16[16,8,2176]{2,1,0:T(8,128)(2,1)}, bf16[512,2816]{1,0:T(8,128)(2,1)S(1)}) custom-call(s32[8]{0:T(128)} %lengths_ref.1, s32[8]{0:T(128)} %adapters_ref.1, bf16[8,64,512]{2,1,0:T(8,128)(2,1)} %query_ref.1, bf16[8,4096]{1,0:T(8,128)(2,1)} %rotary_ref.1, bf16[8,256,512]{2,1,0:T(8,128)(2,1)} %cache_ref.1, bf16[8,64,256]{2,1,0:T(8,128)(2,1)} %keys_ref.1, ...), custom_call_target="tpu_custom_call" | custom-call | tf_op jit(solution)/shard_map/attention/pallas_call | solution.py:119
  6.3 6.8 %all-to-all-start = ((bf16[16,8,2176]{2,1,0:T(8,128)(2,1)}), bf16[16,8,2176]{2,1,0:T(8,128)(2,1)S(1)}, u32[]{:S(2)}, u32[]{:S(2)}) async-start(bf16[16,8,2176]{2,1,0:T(8,128)(2,1)} %get-tuple-element.17), calls=%async_computation | async-start | bytes 1114112 | tf_op jit(solution)/shard_map/all_to_all | solution.py:414
  13.1 1.9 %collective-permute-start.5 = (bf16[64,7168]{1,0:T(8,128)(2,1)}, bf16[64,7168]{1,0:T(8,128)(2,1)}, u32[]{:S(2)}, u32[]{:S(2)}) collective-permute-start(bf16[64,7168]{1,0:T(8,128)(2,1)} %bitcast.4), channel_id=1, source_target_pairs={{0,16},{1,49},{2,18},{3,51},{4,20},{5,53},{6,22},{7,55},{8,24},{9,... | collective-permute-start | bytes 2752520 | tf_op jit(solution)/shard_map/ppermute | solution.py:396
  15.0 0.0 collective-permute-done.3.refs_1_
  15.0 0.0 collective-permute-start.4
  15.0 9.1 %all-to-all-done = bf16[16,8,2176]{2,1,0:T(8,128)(2,1)S(1)} async-done(((bf16[16,8,2176]{2,1,0:T(8,128)(2,1)}), bf16[16,8,2176]{2,1,0:T(8,128)(2,1)S(1)}, u32[]{:S(2)}, u32[]{:S(2)}) %all-to-all-start) | async-done | bytes 557088 | tf_op jit(solution)/shard_map/all_to_all | solution.py:414
  24.1 3.3 %project.1 = (f32[16,4,128]{2,1,0:T(4,128)S(1)}, f32[8,128]{1,0:T(8,128)S(1)}, f32[32,7168]{1,0:T(8,128)S(1)}, bf16[32,7168]{1,0:T(8,128)(2,1)S(1)}, bf16[32,716...) custom-call(bf16[128,2176]{1,0:T(8,128)(2,1)S(1)} %bitcast.2, bf16[512,2816]{1,0:T(8,128)(2,1)S(1)} %get-tuple-element.18.first_tile, ...), custom_call_target="tpu_custom_call" | custom-call | tf_op jit(solution)/shard_map/project/pallas_call | solution.py:284
  27.4 0.5 collective-permute-start
  27.9 2.8 %collective-permute-start.1 = (bf16[32,7168]{1,0:T(8,128)(2,1)S(1)}, bf16[32,7168]{1,0:T(8,128)(2,1)S(1)}, u32[]{:S(2)}, u32[]{:S(2)}) collective-permute-start(bf16[32,7168]{1,0:T(8,128)(2,1)S(1)} %get-tuple-element.23), channel_id=1, source_target_pairs={{0,192},{1,65},{2,194},{3,67},{4,196},{5,69},{6,198},{7,71},{8,200... | collective-permute-start | bytes 1376264 | tf_op jit(solution)/shard_map/ppermute | solution.py:396
  30.8 0.6 %collective-permute-start.2 = (bf16[32,7168]{1,0:T(8,128)(2,1)S(1)}, bf16[32,7168]{1,0:T(8,128)(2,1)S(1)}, u32[]{:S(2)}, u32[]{:S(2)}) collective-permute-start(bf16[32,7168]{1,0:T(8,128)(2,1)S(1)} %get-tuple-element.24), channel_id=1, source_target_pairs={{0,16},{1,193},{2,18},{3,195},{4,20},{5,197},{6,22},{7,199},{8,24}... | collective-permute-start | bytes 1376264 | tf_op jit(solution)/shard_map/ppermute | solution.py:396
  31.3 10.8 %all_to_all.10.low_ref = f32[16,4,128]{2,1,0:T(4,128)S(1)} all-to-all(f32[16,4,128]{2,1,0:T(4,128)S(1)} %get-tuple-element.19), channel_id=1, replica_groups=mesh['dp'=16,'rep'=16] {'dp'}, dimensions={0} | all-to-all | bytes 65536 | tf_op jit(solution)/shard_map/all_to_all | solution.py:424
  42.1 0.0 collective-permute-done.5.refs_3_
  42.1 0.0 collective-permute-done.first_ref
  42.1 0.0 collective-permute-done.1.second_ref
  42.2 0.0 collective-permute-done.4.refs_2_
  42.2 2.5 %adapt.1 = (bf16[8,7168]{1,0:T(8,128)(2,1)S(1)}, bf16[8,7168]{1,0:T(8,128)(2,1)S(1)}, bf16[8,7168]{1,0:T(8,128)(2,1)S(1)}, bf16[8,7168]{1,0:T(8,128)(2,1)S(1)}) custom-call(f32[16,4,128]{2,1,0:T(4,128)S(1)} %all_to_all.10.low_ref, f32[8,128]{1,0:T(8,128)S(1)} %get-tuple-element.20.ids_ref, f32[32,7168]{1,0:T(8,128)S(1)} %get-tuple-element.21.own_ref, ...), custom_call_target="tpu_custom_call" | custom-call | tf_op jit(solution)/shard_map/adapt/pallas_call | solution.py:357
  44.7 1.3 %collective-permute-start.6 = (bf16[8,7168]{1,0:T(8,128)(2,1)S(1)}, bf16[8,7168]{1,0:T(8,128)(2,1)S(1)}, u32[]{:S(2)}, u32[]{:S(2)}) collective-permute-start(bf16[8,7168]{1,0:T(8,128)(2,1)S(1)} %get-tuple-element.26), channel_id=1, source_target_pairs={{0,144},{16,128},{32,176},{48,160},{64,208},{80,192},{96,240},{112... | collective-permute-start | bytes 344072 | tf_op jit(solution)/shard_map/ppermute | solution.py:428
  46.0 3.0 %collective-permute-start.7 = (bf16[8,7168]{1,0:T(8,128)(2,1)S(1)}, bf16[8,7168]{1,0:T(8,128)(2,1)S(1)}, u32[]{:S(2)}, u32[]{:S(2)}) collective-permute-start(bf16[8,7168]{1,0:T(8,128)(2,1)S(1)} %get-tuple-element.27), channel_id=1, source_target_pairs={{0,176},{16,160},{32,144},{48,128},{64,240},{80,224},{96,208},{112... | collective-permute-start | bytes 344072 | tf_op jit(solution)/shard_map/ppermute | solution.py:428
  49.0 2.3 %collective-permute-start.8 = (bf16[8,7168]{1,0:T(8,128)(2,1)S(1)}, bf16[8,7168]{1,0:T(8,128)(2,1)S(1)}, u32[]{:S(2)}, u32[]{:S(2)}) collective-permute-start(bf16[8,7168]{1,0:T(8,128)(2,1)S(1)} %get-tuple-element.28), channel_id=1, source_target_pairs={{0,32},{16,48},{32,0},{48,16},{64,96},{80,112},{96,64},{112,80},{1... | collective-permute-start | bytes 344072 | tf_op jit(solution)/shard_map/ppermute | solution.py:428
  51.3 0.7 %collective-permute-done.6 = bf16[8,7168]{1,0:T(8,128)(2,1)S(1)} collective-permute-done((bf16[8,7168]{1,0:T(8,128)(2,1)S(1)}, bf16[8,7168]{1,0:T(8,128)(2,1)S(1)}, u32[]{:S(2)}, u32[]{:S(2)}) %collective-permute-start.6) | collective-permute-done | bytes 114720 | tf_op jit(solution)/shard_map/ppermute | solution.py:428
  52.0 2.4 %collective-permute-done.7 = bf16[8,7168]{1,0:T(8,128)(2,1)S(1)} collective-permute-done((bf16[8,7168]{1,0:T(8,128)(2,1)S(1)}, bf16[8,7168]{1,0:T(8,128)(2,1)S(1)}, u32[]{:S(2)}, u32[]{:S(2)}) %collective-permute-start.7) | collective-permute-done | bytes 114720 | tf_op jit(solution)/shard_map/ppermute | solution.py:428
  54.4 0.9 %collective-permute-done.8 = bf16[8,7168]{1,0:T(8,128)(2,1)S(1)} collective-permute-done((bf16[8,7168]{1,0:T(8,128)(2,1)S(1)}, bf16[8,7168]{1,0:T(8,128)(2,1)S(1)}, u32[]{:S(2)}, u32[]{:S(2)}) %collective-permute-start.8) | collective-permute-done | bytes 114720 | tf_op jit(solution)/shard_map/ppermute | solution.py:428
  55.3 0.7 %add_convert_fusion = bf16[8,7168]{1,0:T(8,128)(2,1)} fusion(bf16[8,7168]{1,0:T(8,128)(2,1)S(1)} %collective-permute-done.8, bf16[8,7168]{1,0:T(8,128)(2,1)S(1)} %collective-permute-done.7, bf16[8,7168]{1,0:T(8,128)(2,1)S(1)} %collective-permute-done.6, bf16[8,7168]{1,0:T(8,128)(2,1)S(1)} %get-tuple-element.25), kind=kLoop, calls=%fused_computation | loop fusion | flops 458752 | bytes 573440 | tf_op jit(solution)/shard_map/convert_element_type | solution.py:430
  (1 shorter events, 0.0 us)
Async XLA Ops:
  0.0 15.0 %collective-permute-start.3 = (bf16[64,7168]{1,0:T(8,128)(2,1)}, bf16[64,7168]{1,0:T(8,128)(2,1)}, u32[]{:S(2)}, u32[]{:S(2)}) collective-permute-start(bf16[64,7168]{1,0:T(8,128)(2,1)} %bitcast.3), channel_id=1, source_target_pairs={{0,64},{1,193},{2,66},{3,195},{4,68},{5,197},{6,70},{7,199},{8,72}... | collective-permute-start | bytes 2752520 | tf_op jit(solution)/shard_map/ppermute | solution.py:396
  6.3 17.8 %all-to-all-start = ((bf16[16,8,2176]{2,1,0:T(8,128)(2,1)}), bf16[16,8,2176]{2,1,0:T(8,128)(2,1)S(1)}, u32[]{:S(2)}, u32[]{:S(2)}) async-start(bf16[16,8,2176]{2,1,0:T(8,128)(2,1)} %get-tuple-element.17), calls=%async_computation | async-start | bytes 1114112 | tf_op jit(solution)/shard_map/all_to_all | solution.py:414
  13.1 29.0 %collective-permute-start.5 = (bf16[64,7168]{1,0:T(8,128)(2,1)}, bf16[64,7168]{1,0:T(8,128)(2,1)}, u32[]{:S(2)}, u32[]{:S(2)}) collective-permute-start(bf16[64,7168]{1,0:T(8,128)(2,1)} %bitcast.4), channel_id=1, source_target_pairs={{0,16},{1,49},{2,18},{3,51},{4,20},{5,53},{6,22},{7,55},{8,24},{9,... | collective-permute-start | bytes 2752520 | tf_op jit(solution)/shard_map/ppermute | solution.py:396
  15.0 27.1 %collective-permute-start.4 = (bf16[64,7168]{1,0:T(8,128)(2,1)}, bf16[64,7168]{1,0:T(8,128)(2,1)}, u32[]{:S(2)}, u32[]{:S(2)}) collective-permute-start(bf16[64,7168]{1,0:T(8,128)(2,1)} %collective-permute-done.3.refs_1_), channel_id=1, source_target_pairs={{0,1},{1,0},{2,3},{3,2},{4,5},{5,4},{6,7},{7,6},{8,9},{9,8},{10,11... | collective-permute-start | bytes 2752520 | tf_op jit(solution)/shard_map/ppermute | solution.py:396
  27.4 14.7 %collective-permute-start = (bf16[32,7168]{1,0:T(8,128)(2,1)S(1)}, bf16[32,7168]{1,0:T(8,128)(2,1)S(1)}, u32[]{:S(2)}, u32[]{:S(2)}) collective-permute-start(bf16[32,7168]{1,0:T(8,128)(2,1)S(1)} %get-tuple-element.22), channel_id=1, source_target_pairs={{0,64},{1,49},{2,66},{3,51},{4,68},{5,53},{6,70},{7,55},{8,72},{9,... | collective-permute-start | bytes 1376264 | tf_op jit(solution)/shard_map/ppermute | solution.py:396
  27.9 14.2 %collective-permute-start.1 = (bf16[32,7168]{1,0:T(8,128)(2,1)S(1)}, bf16[32,7168]{1,0:T(8,128)(2,1)S(1)}, u32[]{:S(2)}, u32[]{:S(2)}) collective-permute-start(bf16[32,7168]{1,0:T(8,128)(2,1)S(1)} %get-tuple-element.23), channel_id=1, source_target_pairs={{0,192},{1,65},{2,194},{3,67},{4,196},{5,69},{6,198},{7,71},{8,200... | collective-permute-start | bytes 1376264 | tf_op jit(solution)/shard_map/ppermute | solution.py:396
  30.8 11.4 %collective-permute-start.2 = (bf16[32,7168]{1,0:T(8,128)(2,1)S(1)}, bf16[32,7168]{1,0:T(8,128)(2,1)S(1)}, u32[]{:S(2)}, u32[]{:S(2)}) collective-permute-start(bf16[32,7168]{1,0:T(8,128)(2,1)S(1)} %get-tuple-element.24), channel_id=1, source_target_pairs={{0,16},{1,193},{2,18},{3,195},{4,20},{5,197},{6,22},{7,199},{8,24}... | collective-permute-start | bytes 1376264 | tf_op jit(solution)/shard_map/ppermute | solution.py:396
  44.7 7.3 %collective-permute-start.6 = (bf16[8,7168]{1,0:T(8,128)(2,1)S(1)}, bf16[8,7168]{1,0:T(8,128)(2,1)S(1)}, u32[]{:S(2)}, u32[]{:S(2)}) collective-permute-start(bf16[8,7168]{1,0:T(8,128)(2,1)S(1)} %get-tuple-element.26), channel_id=1, source_target_pairs={{0,144},{16,128},{32,176},{48,160},{64,208},{80,192},{96,240},{112... | collective-permute-start | bytes 344072 | tf_op jit(solution)/shard_map/ppermute | solution.py:428
  46.0 8.4 %collective-permute-start.7 = (bf16[8,7168]{1,0:T(8,128)(2,1)S(1)}, bf16[8,7168]{1,0:T(8,128)(2,1)S(1)}, u32[]{:S(2)}, u32[]{:S(2)}) collective-permute-start(bf16[8,7168]{1,0:T(8,128)(2,1)S(1)} %get-tuple-element.27), channel_id=1, source_target_pairs={{0,176},{16,160},{32,144},{48,128},{64,240},{80,224},{96,208},{112... | collective-permute-start | bytes 344072 | tf_op jit(solution)/shard_map/ppermute | solution.py:428
  49.0 6.3 %collective-permute-start.8 = (bf16[8,7168]{1,0:T(8,128)(2,1)S(1)}, bf16[8,7168]{1,0:T(8,128)(2,1)S(1)}, u32[]{:S(2)}, u32[]{:S(2)}) collective-permute-start(bf16[8,7168]{1,0:T(8,128)(2,1)S(1)} %get-tuple-element.28), channel_id=1, source_target_pairs={{0,32},{16,48},{32,0},{48,16},{64,96},{80,112},{96,64},{112,80},{1... | collective-permute-start | bytes 344072 | tf_op jit(solution)/shard_map/ppermute | solution.py:428

commit v6 on v5

--- a/solution.py
+++ b/solution.py
@@ -231,6 +231,22 @@
         )
         for which, part in enumerate(by_class(result)):
             values[which, :, head * width : (head + 1) * width] = part.astype(BF16)
+    steps = [jnp.where(core == 0, *pair) for pair in zip(*SENDING, strict=True)] + [0]
+    ordered = jnp.concatenate(
+        [values[lax.rem(which_own + step, CLASSES)] for step in steps], axis=0
+    )
+
+    def multiply(tile):
+        if tile > 0:
+            copies[1 + tile].wait()
+        part = weight[tile - 1] if tile > 0 else first_tile[...]
+        total = jnp.dot(ordered, part, preferred_element_type=F32)
+        columns = pl.ds(0, STAGED) if tile == 0 else pl.ds(STAGED + (tile - 1) * TILE, TILE)
+        for i, other_ref in enumerate((first_ref, second_ref, third_ref)):
+            other_ref[:, columns] = total[i * own_rows : (i + 1) * own_rows].astype(BF16)
+        own_ref[:, columns] = total[3 * own_rows :]
+
+    multiply(0)
     ids = jnp.concatenate(by_class(gathered_ref[:, heads * latent :].astype(F32)), axis=0)
     copies[1].wait()
     projected = jnp.dot(
@@ -261,20 +277,8 @@
     for which in range(1, CLASSES):
         own_ids = jnp.where(which_own == which, pltpu.roll(ids, turns[which], 1), own_ids)
     ids_ref[...] = own_ids
-
-    steps = [jnp.where(core == 0, *pair) for pair in zip(*SENDING, strict=True)] + [0]
-    ordered = jnp.concatenate(
-        [values[lax.rem(which_own + step, CLASSES)] for step in steps], axis=0
-    )
-    for tile in range(tiles):
-        if tile > 0:
-            copies[1 + tile].wait()
-        part = weight[tile - 1] if tile > 0 else first_tile[...]
-        total = jnp.dot(ordered, part, preferred_element_type=F32)
-        columns = pl.ds(0, STAGED) if tile == 0 else pl.ds(STAGED + (tile - 1) * TILE, TILE)
-        for i, other_ref in enumerate((first_ref, second_ref, third_ref)):
-            other_ref[:, columns] = total[i * own_rows : (i + 1) * own_rows].astype(BF16)
-        own_ref[:, columns] = total[3 * own_rows :]
+    for tile in range(1, tiles):
+        multiply(tile)
 
 
 def project(gathered, first_tile, value_up, down, weight):

time: 56.3 us -> 56.6 us (level)
  transfers between devices with their start and end apart: 10 -> 10, of which waited for: 4 -> 4; matrix products, arithmetic and copies ran while one was open for 0% -> 0% of each run, Pallas kernels for 14% -> 15%
where the time goes in v6:
time: 56.6 us; the launch traced here: 56.3 us
  starting transfers between devices  20.7 us (37%)
  waiting for transfers between devices  13.1 us (23%)
  Pallas kernels  10.9 us (19%)
  blocking collectives  10.8 us (19%)
  other arithmetic  0.71 us (1%)
    all_to_all x1, blocking collectives, on_device(): low = exchange(low)  10.8 us
    all_to_all x1, waiting for transfers between devices, on_device(): gathered = exchange(message)  9.09 us
    ppermute x6, starting transfers between devices, swap(): return lax.ppermute(array, ('dp', 'rep'), perm)  7.38 us
    all_to_all x1, starting transfers between devices, on_device(): gathered = exchange(message)  6.76 us
    ppermute x3, starting transfers between devices, on_device(): part = lax.ppermute(part, 'dp', [(i, i ^ bits) for i in range(GROUPS)])  6.58 us
    pallas_call x1, Pallas kernels, attention(): pl.pallas_call(attention_kernel, grid=(req_local // per_step,), in_specs=...  4.76 us
    ppermute x3, waiting for transfers between devices, on_device(): part = lax.ppermute(part, 'dp', [(i, i ^ bits) for i in range(GROUPS)])  4.02 us
    pallas_call x1, Pallas kernels, project(): pl.pallas_call(project_kernel, in_specs=[in_vmem] * 2 + [pl.BlockSpec(mem...  3.61 us
  transfers between devices with their start and end apart: 10, of which 4 were waited for; matrix products, arithmetic and copies ran while one was open for 0% of the time, Pallas kernels for 15%

profile of v6, /device:TPU:160, one launch (start us, length us, event | category | flops | bytes accessed | tf_op | source)
XLA Modules:
  0.0 56.3 jit_solution(6247516796087282381)
XLA Ops:
  0.0 1.6 %collective-permute-start.3 = (bf16[64,7168]{1,0:T(8,128)(2,1)}, bf16[64,7168]{1,0:T(8,128)(2,1)}, u32[]{:S(2)}, u32[]{:S(2)}) collective-permute-start(bf16[64,7168]{1,0:T(8,128)(2,1)} %bitcast.3), channel_id=1, source_target_pairs={{0,64},{1,193},{2,66},{3,195},{4,68},{5,197},{6,70},{7,199},{8,72}... | collective-permute-start | bytes 2752520 | tf_op jit(solution)/shard_map/ppermute | solution.py:400
  1.6 4.8 %attention.1 = (bf16[16,8,2176]{2,1,0:T(8,128)(2,1)}, bf16[512,2816]{1,0:T(8,128)(2,1)S(1)}) custom-call(s32[8]{0:T(128)} %lengths_ref.1, s32[8]{0:T(128)} %adapters_ref.1, bf16[8,64,512]{2,1,0:T(8,128)(2,1)} %query_ref.1, bf16[8,4096]{1,0:T(8,128)(2,1)} %rotary_ref.1, bf16[8,256,512]{2,1,0:T(8,128)(2,1)} %cache_ref.1, bf16[8,64,256]{2,1,0:T(8,128)(2,1)} %keys_ref.1, ...), custom_call_target="tpu_custom_call" | custom-call | tf_op jit(solution)/shard_map/attention/pallas_call | solution.py:119
  6.3 6.8 %all-to-all-start = ((bf16[16,8,2176]{2,1,0:T(8,128)(2,1)}), bf16[16,8,2176]{2,1,0:T(8,128)(2,1)S(1)}, u32[]{:S(2)}, u32[]{:S(2)}) async-start(bf16[16,8,2176]{2,1,0:T(8,128)(2,1)} %get-tuple-element.17), calls=%async_computation | async-start | bytes 1114112 | tf_op jit(solution)/shard_map/all_to_all | solution.py:418
  13.1 1.9 %collective-permute-start.5 = (bf16[64,7168]{1,0:T(8,128)(2,1)}, bf16[64,7168]{1,0:T(8,128)(2,1)}, u32[]{:S(2)}, u32[]{:S(2)}) collective-permute-start(bf16[64,7168]{1,0:T(8,128)(2,1)} %bitcast.4), channel_id=1, source_target_pairs={{0,16},{1,49},{2,18},{3,51},{4,20},{5,53},{6,22},{7,55},{8,24},{9,... | collective-permute-start | bytes 2752520 | tf_op jit(solution)/shard_map/ppermute | solution.py:400
  15.0 0.0 collective-permute-done.3.refs_1_
  15.0 0.0 collective-permute-start.4
  15.0 9.1 %all-to-all-done = bf16[16,8,2176]{2,1,0:T(8,128)(2,1)S(1)} async-done(((bf16[16,8,2176]{2,1,0:T(8,128)(2,1)}), bf16[16,8,2176]{2,1,0:T(8,128)(2,1)S(1)}, u32[]{:S(2)}, u32[]{:S(2)}) %all-to-all-start) | async-done | bytes 557088 | tf_op jit(solution)/shard_map/all_to_all | solution.py:418
  24.1 3.6 %project.1 = (f32[16,4,128]{2,1,0:T(4,128)S(1)}, f32[8,128]{1,0:T(8,128)S(1)}, f32[32,7168]{1,0:T(8,128)S(1)}, bf16[32,7168]{1,0:T(8,128)(2,1)S(1)}, bf16[32,716...) custom-call(bf16[128,2176]{1,0:T(8,128)(2,1)S(1)} %bitcast.2, bf16[512,2816]{1,0:T(8,128)(2,1)S(1)} %get-tuple-element.18.first_tile, ...), custom_call_target="tpu_custom_call" | custom-call | tf_op jit(solution)/shard_map/project/pallas_call | solution.py:288
  27.7 0.5 collective-permute-start
  28.2 2.9 %collective-permute-start.1 = (bf16[32,7168]{1,0:T(8,128)(2,1)S(1)}, bf16[32,7168]{1,0:T(8,128)(2,1)S(1)}, u32[]{:S(2)}, u32[]{:S(2)}) collective-permute-start(bf16[32,7168]{1,0:T(8,128)(2,1)S(1)} %get-tuple-element.23), channel_id=1, source_target_pairs={{0,192},{1,65},{2,194},{3,67},{4,196},{5,69},{6,198},{7,71},{8,200... | collective-permute-start | bytes 1376264 | tf_op jit(solution)/shard_map/ppermute | solution.py:400
  31.1 0.6 collective-permute-start.2
  31.6 10.8 %all_to_all.10.low_ref = f32[16,4,128]{2,1,0:T(4,128)S(1)} all-to-all(f32[16,4,128]{2,1,0:T(4,128)S(1)} %get-tuple-element.19), channel_id=1, replica_groups=mesh['dp'=16,'rep'=16] {'dp'}, dimensions={0} | all-to-all | bytes 65536 | tf_op jit(solution)/shard_map/all_to_all | solution.py:428
  42.4 0.0 collective-permute-done.5.refs_3_
  42.4 0.0 collective-permute-done.first_ref
  42.4 0.0 collective-permute-done.1.second_ref
  42.4 0.0 collective-permute-done.2.third_ref
  42.5 2.5 %adapt.1 = (bf16[8,7168]{1,0:T(8,128)(2,1)S(1)}, bf16[8,7168]{1,0:T(8,128)(2,1)S(1)}, bf16[8,7168]{1,0:T(8,128)(2,1)S(1)}, bf16[8,7168]{1,0:T(8,128)(2,1)S(1)}) custom-call(f32[16,4,128]{2,1,0:T(4,128)S(1)} %all_to_all.10.low_ref, f32[8,128]{1,0:T(8,128)S(1)} %get-tuple-element.20.ids_ref, f32[32,7168]{1,0:T(8,128)S(1)} %get-tuple-element.21.own_ref, ...), custom_call_target="tpu_custom_call" | custom-call | tf_op jit(solution)/shard_map/adapt/pallas_call | solution.py:361
  45.0 1.3 %collective-permute-start.6 = (bf16[8,7168]{1,0:T(8,128)(2,1)S(1)}, bf16[8,7168]{1,0:T(8,128)(2,1)S(1)}, u32[]{:S(2)}, u32[]{:S(2)}) collective-permute-start(bf16[8,7168]{1,0:T(8,128)(2,1)S(1)} %get-tuple-element.26), channel_id=1, source_target_pairs={{0,144},{16,128},{32,176},{48,160},{64,208},{80,192},{96,240},{112... | collective-permute-start | bytes 344072 | tf_op jit(solution)/shard_map/ppermute | solution.py:432
  46.3 3.0 %collective-permute-start.7 = (bf16[8,7168]{1,0:T(8,128)(2,1)S(1)}, bf16[8,7168]{1,0:T(8,128)(2,1)S(1)}, u32[]{:S(2)}, u32[]{:S(2)}) collective-permute-start(bf16[8,7168]{1,0:T(8,128)(2,1)S(1)} %get-tuple-element.27), channel_id=1, source_target_pairs={{0,176},{16,160},{32,144},{48,128},{64,240},{80,224},{96,208},{112... | collective-permute-start | bytes 344072 | tf_op jit(solution)/shard_map/ppermute | solution.py:432
  49.3 2.3 %collective-permute-start.8 = (bf16[8,7168]{1,0:T(8,128)(2,1)S(1)}, bf16[8,7168]{1,0:T(8,128)(2,1)S(1)}, u32[]{:S(2)}, u32[]{:S(2)}) collective-permute-start(bf16[8,7168]{1,0:T(8,128)(2,1)S(1)} %get-tuple-element.28), channel_id=1, source_target_pairs={{0,32},{16,48},{32,0},{48,16},{64,96},{80,112},{96,64},{112,80},{1... | collective-permute-start | bytes 344072 | tf_op jit(solution)/shard_map/ppermute | solution.py:432
  51.6 0.7 %collective-permute-done.6 = bf16[8,7168]{1,0:T(8,128)(2,1)S(1)} collective-permute-done((bf16[8,7168]{1,0:T(8,128)(2,1)S(1)}, bf16[8,7168]{1,0:T(8,128)(2,1)S(1)}, u32[]{:S(2)}, u32[]{:S(2)}) %collective-permute-start.6) | collective-permute-done | bytes 114720 | tf_op jit(solution)/shard_map/ppermute | solution.py:432
  52.3 2.4 %collective-permute-done.7 = bf16[8,7168]{1,0:T(8,128)(2,1)S(1)} collective-permute-done((bf16[8,7168]{1,0:T(8,128)(2,1)S(1)}, bf16[8,7168]{1,0:T(8,128)(2,1)S(1)}, u32[]{:S(2)}, u32[]{:S(2)}) %collective-permute-start.7) | collective-permute-done | bytes 114720 | tf_op jit(solution)/shard_map/ppermute | solution.py:432
  54.7 0.9 %collective-permute-done.8 = bf16[8,7168]{1,0:T(8,128)(2,1)S(1)} collective-permute-done((bf16[8,7168]{1,0:T(8,128)(2,1)S(1)}, bf16[8,7168]{1,0:T(8,128)(2,1)S(1)}, u32[]{:S(2)}, u32[]{:S(2)}) %collective-permute-start.8) | collective-permute-done | bytes 114720 | tf_op jit(solution)/shard_map/ppermute | solution.py:432
  55.6 0.7 %add_convert_fusion = bf16[8,7168]{1,0:T(8,128)(2,1)} fusion(bf16[8,7168]{1,0:T(8,128)(2,1)S(1)} %collective-permute-done.8, bf16[8,7168]{1,0:T(8,128)(2,1)S(1)} %collective-permute-done.7, bf16[8,7168]{1,0:T(8,128)(2,1)S(1)} %collective-permute-done.6, bf16[8,7168]{1,0:T(8,128)(2,1)S(1)} %get-tuple-element.25), kind=kLoop, calls=%fused_computation | loop fusion | flops 458752 | bytes 573440 | tf_op jit(solution)/shard_map/convert_element_type | solution.py:434
  (1 shorter events, 0.0 us)
Async XLA Ops:
  0.0 15.0 %collective-permute-start.3 = (bf16[64,7168]{1,0:T(8,128)(2,1)}, bf16[64,7168]{1,0:T(8,128)(2,1)}, u32[]{:S(2)}, u32[]{:S(2)}) collective-permute-start(bf16[64,7168]{1,0:T(8,128)(2,1)} %bitcast.3), channel_id=1, source_target_pairs={{0,64},{1,193},{2,66},{3,195},{4,68},{5,197},{6,70},{7,199},{8,72}... | collective-permute-start | bytes 2752520 | tf_op jit(solution)/shard_map/ppermute | solution.py:400
  6.3 17.8 %all-to-all-start = ((bf16[16,8,2176]{2,1,0:T(8,128)(2,1)}), bf16[16,8,2176]{2,1,0:T(8,128)(2,1)S(1)}, u32[]{:S(2)}, u32[]{:S(2)}) async-start(bf16[16,8,2176]{2,1,0:T(8,128)(2,1)} %get-tuple-element.17), calls=%async_computation | async-start | bytes 1114112 | tf_op jit(solution)/shard_map/all_to_all | solution.py:418
  13.1 29.3 %collective-permute-start.5 = (bf16[64,7168]{1,0:T(8,128)(2,1)}, bf16[64,7168]{1,0:T(8,128)(2,1)}, u32[]{:S(2)}, u32[]{:S(2)}) collective-permute-start(bf16[64,7168]{1,0:T(8,128)(2,1)} %bitcast.4), channel_id=1, source_target_pairs={{0,16},{1,49},{2,18},{3,51},{4,20},{5,53},{6,22},{7,55},{8,24},{9,... | collective-permute-start | bytes 2752520 | tf_op jit(solution)/shard_map/ppermute | solution.py:400
  15.0 27.4 %collective-permute-start.4 = (bf16[64,7168]{1,0:T(8,128)(2,1)}, bf16[64,7168]{1,0:T(8,128)(2,1)}, u32[]{:S(2)}, u32[]{:S(2)}) collective-permute-start(bf16[64,7168]{1,0:T(8,128)(2,1)} %collective-permute-done.3.refs_1_), channel_id=1, source_target_pairs={{0,1},{1,0},{2,3},{3,2},{4,5},{5,4},{6,7},{7,6},{8,9},{9,8},{10,11... | collective-permute-start | bytes 2752520 | tf_op jit(solution)/shard_map/ppermute | solution.py:400
  27.7 14.7 %collective-permute-start = (bf16[32,7168]{1,0:T(8,128)(2,1)S(1)}, bf16[32,7168]{1,0:T(8,128)(2,1)S(1)}, u32[]{:S(2)}, u32[]{:S(2)}) collective-permute-start(bf16[32,7168]{1,0:T(8,128)(2,1)S(1)} %get-tuple-element.22), channel_id=1, source_target_pairs={{0,64},{1,49},{2,66},{3,51},{4,68},{5,53},{6,70},{7,55},{8,72},{9,... | collective-permute-start | bytes 1376264 | tf_op jit(solution)/shard_map/ppermute | solution.py:400
  28.2 14.2 %collective-permute-start.1 = (bf16[32,7168]{1,0:T(8,128)(2,1)S(1)}, bf16[32,7168]{1,0:T(8,128)(2,1)S(1)}, u32[]{:S(2)}, u32[]{:S(2)}) collective-permute-start(bf16[32,7168]{1,0:T(8,128)(2,1)S(1)} %get-tuple-element.23), channel_id=1, source_target_pairs={{0,192},{1,65},{2,194},{3,67},{4,196},{5,69},{6,198},{7,71},{8,200... | collective-permute-start | bytes 1376264 | tf_op jit(solution)/shard_map/ppermute | solution.py:400
  31.1 11.4 %collective-permute-start.2 = (bf16[32,7168]{1,0:T(8,128)(2,1)S(1)}, bf16[32,7168]{1,0:T(8,128)(2,1)S(1)}, u32[]{:S(2)}, u32[]{:S(2)}) collective-permute-start(bf16[32,7168]{1,0:T(8,128)(2,1)S(1)} %get-tuple-element.24), channel_id=1, source_target_pairs={{0,16},{1,193},{2,18},{3,195},{4,20},{5,197},{6,22},{7,199},{8,24}... | collective-permute-start | bytes 1376264 | tf_op jit(solution)/shard_map/ppermute | solution.py:400
  45.0 7.3 %collective-permute-start.6 = (bf16[8,7168]{1,0:T(8,128)(2,1)S(1)}, bf16[8,7168]{1,0:T(8,128)(2,1)S(1)}, u32[]{:S(2)}, u32[]{:S(2)}) collective-permute-start(bf16[8,7168]{1,0:T(8,128)(2,1)S(1)} %get-tuple-element.26), channel_id=1, source_target_pairs={{0,144},{16,128},{32,176},{48,160},{64,208},{80,192},{96,240},{112... | collective-permute-start | bytes 344072 | tf_op jit(solution)/shard_map/ppermute | solution.py:432
  46.3 8.4 %collective-permute-start.7 = (bf16[8,7168]{1,0:T(8,128)(2,1)S(1)}, bf16[8,7168]{1,0:T(8,128)(2,1)S(1)}, u32[]{:S(2)}, u32[]{:S(2)}) collective-permute-start(bf16[8,7168]{1,0:T(8,128)(2,1)S(1)} %get-tuple-element.27), channel_id=1, source_target_pairs={{0,176},{16,160},{32,144},{48,128},{64,240},{80,224},{96,208},{112... | collective-permute-start | bytes 344072 | tf_op jit(solution)/shard_map/ppermute | solution.py:432
  49.3 6.3 %collective-permute-start.8 = (bf16[8,7168]{1,0:T(8,128)(2,1)S(1)}, bf16[8,7168]{1,0:T(8,128)(2,1)S(1)}, u32[]{:S(2)}, u32[]{:S(2)}) collective-permute-start(bf16[8,7168]{1,0:T(8,128)(2,1)S(1)} %get-tuple-element.28), channel_id=1, source_target_pairs={{0,32},{16,48},{32,0},{48,16},{64,96},{80,112},{96,64},{112,80},{1... | collective-permute-start | bytes 344072 | tf_op jit(solution)/shard_map/ppermute | solution.py:432
